TPU v7x, 256 devices: a whole 4x4x8 slice. The times are simulated.
256 devices in a mesh: scan: 16 (over y, x), chan: 16 (over z, core).
Axes of the slice: x: 4, y: 4, z: 8, core: 2. Of those that a mesh axis runs over, the one named last changes fastest.
Arguments:
- spectra: bfloat16 [16384, 4096], P('scan', 'chan'), may hold values from -48 to 48
- chan_weight: bfloat16 [16384, 4096], P('scan', 'chan'), may hold values from 0.25 to 4
- kernel: bfloat16 [16384, 128], P('scan'), may hold values from 0.019897461 to 1
- tile_map: int32 [16384], P('scan'), may hold values from 0 to 63, as said below
- tile_slot: int32 [64], replicated, may hold values from 0 to 63, as said below
Outputs:
- baseline_coef: float32 [5, 8192], P(None, ('scan', 'chan'))
- residual: float32 [8192, 4096], P(('scan', 'chan'))
Inputs may be any that keep to these rules, and one draw needn't show every extreme that they name: `tile_map`: each spectrum names one of the 64 tiles; among the spectra of one index of scan at most 128 name tiles of any one owner, and one owner receives exactly 128 from every index of scan. `tile_slot`: every position occurs once; the tiles at positions r * 4 to (r + 1) * 4 - 1 belong to index r of scan.
All inputs are finite; a program needn't handle non-finite values.
Results may differ from a plain program's by a relative error of at most 0.0026.
Values may be sent and summed in bfloat16 or wider, within the bound.
No kernel may reach another device: no remote copies, remote signals or barrier semaphores. Data moves between devices by JAX's collectives and lax.ppermute only.
A program may use at most 64 MiB of HBM per device.

v0:
```python
import jax
import jax.numpy as jnp
from jax import lax
from jax.sharding import PartitionSpec as P

CHANNELS = 4096
BASIS = 5


def basis_table(total, terms):
    abscissa = (2.0 * jnp.arange(total).astype(jnp.float32) + 1.0) / total - 1.0
    columns = []
    for degree in range(terms):
        column = abscissa**degree
        for earlier in columns:
            column = column - jnp.sum(earlier * column) * earlier
        column = column / jnp.sqrt(jnp.sum(column * column))
        columns.append(column)
    return jnp.stack(columns, axis=1)


def slot_lookup(tile_map, tile_slot):
    all_tiles = jnp.arange(tile_slot.shape[0], dtype=jnp.int32)
    matched = tile_map[:, None] == all_tiles[None, :]
    return jnp.sum(jnp.where(matched, tile_slot[None, :], 0), axis=1)


def stack_rows(spectra, chan_weight):
    weighted = (chan_weight.astype(jnp.float32) * spectra.astype(jnp.float32)).astype(jnp.bfloat16)
    return jnp.concatenate([weighted, chan_weight], axis=1)


def grid_block(kernel_cols, stacked, slot_ids, amount):
    wanted = jnp.arange(amount, dtype=jnp.int32)
    selected = slot_ids[None, :] == wanted[:, None]
    masked = jnp.where(
        selected[:, None, :], kernel_cols[None, :, :], jnp.zeros((), kernel_cols.dtype)
    )
    flattened = masked.reshape(amount * kernel_cols.shape[0], kernel_cols.shape[1])
    product = jnp.dot(flattened, stacked, preferred_element_type=jnp.float32)
    return product.reshape(amount, kernel_cols.shape[0], stacked.shape[1])


def per_device(spectra, chan_weight, kernel, tile_map, tile_slot):
    slot_ids = slot_lookup(tile_map, tile_slot)
    tiles_owned = tile_slot.shape[0] // lax.axis_size("scan")
    stacked = stack_rows(spectra, chan_weight)
    kernel_cols = kernel.T
    gridded = lax.psum_scatter(
        grid_block(kernel_cols, stacked, slot_ids, tiles_owned * lax.axis_size("scan")),
        "scan",
        scatter_dimension=0,
        tiled=True,
    )
    block_width = spectra.shape[1]
    grid_cube = (gridded[..., :block_width] / (gridded[..., block_width:] + 1.0)).reshape(
        -1, block_width
    )
    basis = basis_table(CHANNELS, BASIS)
    pixel_rows = lax.all_to_all(grid_cube, "chan", split_axis=0, concat_axis=1, tiled=True)
    coeffs = jnp.einsum("ck,pc->kp", basis, pixel_rows, precision=lax.Precision.HIGHEST)
    residual = pixel_rows - jnp.einsum("ck,kp->pc", basis, coeffs, precision=lax.Precision.HIGHEST)
    return (coeffs, residual)


def solution(mesh):
    placed = (P("scan", "chan"), P("scan", "chan"), P("scan", None), P("scan"), P())
    return jax.shard_map(
        per_device,
        mesh=mesh,
        in_specs=placed,
        out_specs=(P(None, ("scan", "chan")), P(("scan", "chan"), None)),
        check_vma=False,
    )
```

profile of v0, /device:TPU:1, one launch (start us, length us, event | category | flops | bytes accessed | tf_op | source)
XLA Modules:
  0.0 192.3 jit_solution(12513415022376135737)
XLA Ops:
  7.2 0.0 reduce-scatter.2.cloned.1.call-start
  7.2 0.8 select_reduce_fusion
  8.1 1.1 copy.11
  9.2 1.3 multiply_convert_fusion
  10.5 12.4 %fusion = f32[64,128,512]{2,1,0:T(8,128)} fusion(pred[64,1024]{1,0:T(8,128)(4,1)S(1)} %iota_compare_fusion, bf16[128,1024]{1,0:T(8,128)(2,1)S(1)} %copy.11, bf16[1024,256]{1,0:T(8,128)(2,1)} %param.6, bf16[1024,256]{1,0:T(8,128)(2,1)S(1)} %multiply_convert_fusion), kind=kOutput, calls=%fused_computation | convolution fusion | flops 8600420352 | bytes 18153472 | tf_op jit(solution)/shard_map/dot_general | solution.py:40
  22.9 0.0 reduce-scatter.2.cloned.1.call-update
  22.9 119.2 %reduce-scatter.2.cloned.1.call-done = f32[4,128,512]{2,1,0:T(8,128)} async-done(((f32[64,128,512]{2,1,0:T(8,128)}), f32[4,128,512]{2,1,0:T(8,128)}) %reduce-scatter.2.cloned.1.call-update) | async-done | bytes 1048592 | tf_op jit(solution)/shard_map/reduce_scatter | solution.py:49
  142.1 2.1 %fusion.7 = f32[4,128,256]{2,1,0:T(8,128)} fusion(f32[4,128,512]{2,1,0:T(8,128)} %reduce-scatter.2.cloned.1.call-done), kind=kLoop, calls=%fused_computation.11 | loop fusion | flops 262144 | bytes 1572864 | tf_op jit(solution)/shard_map/div | solution.py:56
  144.2 8.1 %all-to-all-start = ((f32[16,32,256]{2,1,0:T(8,128)}), f32[16,32,256]{2,1,0:T(8,128)S(1)}, u32[]{:S(2)}, u32[]{:S(2)}) async-start(f32[16,32,256]{2,1,0:T(8,128)} %bitcast.2), calls=%async_computation.1 | async-start | bytes 1048576 | tf_op jit(solution)/shard_map/all_to_all | solution.py:60
  152.3 0.6 multiply_reduce_fusion.8
  153.6 0.6 fusion.8
  154.8 0.6 multiply_reduce_fusion.12
  156.1 0.6 multiply_reduce_fusion.11
  157.4 0.6 multiply_reduce_fusion.10
  158.0 1.3 multiply_reduce_fusion.9
  160.1 0.7 multiply_reduce_fusion.7
  160.8 1.9 %multiply_reduce_fusion.6 = f32[]{:T(128)} fusion(f32[]{:T(128)S(6)} %sqrt.14, f32[]{:T(128)S(6)} %sqrt.13, f32[]{:T(128)S(6)} %mul.252, f32[]{:T(128)} %multiply_reduce_fusion.10, f32[]{:T(128)S(6)} %mul.255, f32[]{:T(128)} %multiply_reduce_fusion.7, f32[]{:T(128)S(6)} %mul.263), kind=kLoop, calls=%fused_computation.31 | loop fusion | flops 73727 | bytes 32 | tf_op jit(solution)/shard_map/reduce_sum | solution.py:16
  162.7 2.5 %multiply_reduce_fusion.5 = f32[]{:T(128)} fusion(f32[]{:T(128)S(6)} %sqrt.14, f32[]{:T(128)} %multiply_reduce_fusion.10, f32[]{:T(128)S(6)} %mul.255, f32[]{:T(128)} %multiply_reduce_fusion.6, f32[]{:T(128)S(6)} %sqrt.13, f32[]{:T(128)S(6)} %mul.252, f32[]{:T(128)} %multiply_reduce_fusion.7, f32[]{:T(128)S(6)} %mul.263), kind=kLoop, calls=%fused_computation.28 | loop fusion | flops 81919 | bytes 36 | tf_op jit(solution)/shard_map/reduce_sum | solution.py:17
  165.9 0.6 multiply_reduce_fusion.4
  167.2 0.6 multiply_reduce_fusion.3
  167.9 2.0 %multiply_reduce_fusion.2 = f32[]{:T(128)} fusion(f32[]{:T(128)S(6)} %sqrt.14, f32[]{:T(128)S(6)} %sqrt.13, f32[]{:T(128)S(6)} %mul.252, f32[]{:T(128)} %multiply_reduce_fusion.10, f32[]{:T(128)S(6)} %mul.255, f32[]{:T(128)} %multiply_reduce_fusion.3, f32[]{:T(128)S(6)} %mul.278), kind=kLoop, calls=%fused_computation.24 | loop fusion | flops 73727 | bytes 32 | tf_op jit(solution)/shard_map/reduce_sum | solution.py:16
  169.8 3.8 %multiply_reduce_fusion.1 = f32[]{:T(128)} fusion(f32[]{:T(128)S(6)} %sqrt.14, f32[]{:T(128)} %multiply_reduce_fusion.10, f32[]{:T(128)S(6)} %mul.255, f32[]{:T(128)} %multiply_reduce_fusion.2, f32[]{:T(128)S(6)} %sqrt.13, f32[]{:T(128)S(6)} %mul.252, f32[]{:T(128)} %multiply_reduce_fusion.3, f32[]{:T(128)S(6)} %mul.278, f32[]{:T(128)S(6)} %sqrt.15, ...), kind=kLoop, calls=%fused_computation.22 | loop fusion | flops 110591 | bytes 52 | tf_op jit(solution)/shard_map/reduce_sum | solution.py:16
  173.6 4.4 %multiply_reduce_fusion = f32[]{:T(128)} fusion(f32[]{:T(128)} %multiply_reduce_fusion.1, f32[]{:T(128)S(6)} %sqrt.14, f32[]{:T(128)} %multiply_reduce_fusion.10, f32[]{:T(128)S(6)} %mul.255, f32[]{:T(128)} %multiply_reduce_fusion.2, f32[]{:T(128)S(6)} %sqrt.13, f32[]{:T(128)S(6)} %mul.252, f32[]{:T(128)} %multiply_reduce_fusion.3, f32[]{:T(128)S(6)} %mul.278, ...), kind=kLoop, calls=%fused_computation.20 | loop fusion | flops 118783 | bytes 56 | tf_op jit(solution)/shard_map/reduce_sum | solution.py:17
  178.7 0.7 subtract_divide_fusion.2
  179.4 3.9 %subtract_divide_fusion = (f32[4096,1]{0,1:T(1,128)S(1)}, f32[4096,1]{0,1:T(1,128)S(1)}) fusion(f32[]{:T(128)S(6)} %sqrt.16, f32[]{:T(128)} %multiply_reduce_fusion.1, f32[]{:T(128)} %multiply_reduce_fusion.2, f32[]{:T(128)} %multiply_reduce_fusion.3, f32[]{:T(128)S(6)} %mul.278, f32[]{:T(128)S(6)} %sqrt.13, f32[]{:T(128)S(6)} %mul.252, f32[]{:T(128)S(6)} %sqrt.14, ...), kind=kLoop, calls=%fused_computation.21 | loop fusion | flops 114688 | bytes 32824 | tf_op jit(solution)/shard_map/div | solution.py:17
  183.3 0.1 stack.5
  183.4 0.0 all-to-all-done
  183.5 0.5 fusion.16
  184.0 0.0 copy-start
  184.0 1.5 convolution_subtract_fusion
  185.5 0.0 copy-done
  (3 shorter events, 0.1 us)
Async XLA Ops:
  7.2 135.0 %reduce-scatter.2.cloned.1.call-start = ((), (), s32[]{:S(2)}) async-start(), calls=%async_computation.2 | async-start | bytes 17825792 | tf_op jit(solution)/shard_map/reduce_scatter | solution.py:49
  144.2 39.2 %all-to-all-start = ((f32[16,32,256]{2,1,0:T(8,128)}), f32[16,32,256]{2,1,0:T(8,128)S(1)}, u32[]{:S(2)}, u32[]{:S(2)}) async-start(f32[16,32,256]{2,1,0:T(8,128)} %bitcast.2), calls=%async_computation.1 | async-start | bytes 1048576 | tf_op jit(solution)/shard_map/all_to_all | solution.py:60
  184.0 1.5 copy-start
Sparse Core Ops, SparseCore 0:
  23.1 119.0 reduce-scatter.1
where the time goes:
time: 193 us; the launch traced here: 192 us
  waiting for transfers between devices  119 us (62%)
  other arithmetic  29.9 us (15%)
  between operations  19.5 us (10%)
  matrix products  14.4 us (7%)
  starting transfers between devices  8.12 us (4%)
    reduce_scatter x1, waiting for transfers between devices, per_device(): lax.psum_scatter(grid_block(kernel_cols, stacked, slot_ids, tiles_owned *...  119 us
    dot_general x1, matrix products, grid_block(): product = jnp.dot(flattened, stacked, preferred_element_type=jnp.float32)  12.4 us
    reduce_sum x10, other arithmetic, basis_table(): column = column - jnp.sum(earlier * column) * earlier  12.1 us
    reduce_sum x4, other arithmetic, basis_table(): column = column / jnp.sqrt(jnp.sum(column * column))  8.87 us
    all_to_all x1, starting transfers between devices, per_device(): lax.all_to_all(grid_cube, 'chan', split_axis=0, concat_axis=1, tiled=True)  8.08 us
    div x2, other arithmetic, basis_table(): column = column / jnp.sqrt(jnp.sum(column * column))  4.61 us
  transfers between devices with their start and end apart: 2, of which 1 were waited for; matrix products, arithmetic and copies ran while one was open for 13% of the time, Pallas kernels for 0%

commit v1 on v0

v1 whole, which is shorter than its diff:
```python
import functools

import jax
import jax.numpy as jnp
import numpy as np
from jax import lax
from jax.experimental import pallas as pl
from jax.experimental.pallas import tpu as pltpu
from jax.sharding import PartitionSpec as P

CHANNELS = 4096
BASIS = 5
CAP = 128
TILES = 4
LANES = 128
HIGHEST = lax.Precision.HIGHEST


def orthonormal(abscissa, terms):
    columns = []
    for degree in range(terms):
        column = abscissa**degree
        for earlier in columns:
            column = column - np.sum(earlier * column) * earlier
        columns.append(column / np.sqrt(np.sum(column * column)))
    return np.stack(columns, axis=1)


def tables(channels, parts):
    width = channels // parts
    basis = orthonormal((2.0 * np.arange(channels) + 1.0) / channels - 1.0, BASIS)
    local = orthonormal((2.0 * np.arange(width) + 1.0) / width - 1.0, BASIS)
    mix = np.stack([local.T @ basis[c * width : (c + 1) * width] for c in range(parts)])
    project = np.zeros((width, LANES))
    for copy in range(3):
        project[:, copy * BASIS : (copy + 1) * BASIS] = local
    expand = np.zeros((LANES, width))
    expand[:BASIS] = local.T
    combine = np.zeros((parts * 8 + 8, parts * 16))
    for c in range(parts):
        for copy in range(3):
            at = c * 16 + copy * BASIS
            combine[parts * 8 : parts * 8 + BASIS, at : at + BASIS] = mix[c].T
            combine[c * 8 : c * 8 + BASIS, at : at + BASIS] += np.eye(BASIS)
    for c in range(parts):
        combine[c * 8 : c * 8 + BASIS] -= mix[c] @ combine[parts * 8 : parts * 8 + BASIS]
    short = np.zeros((8, width))
    short[:BASIS] = local.T
    return [a.astype(np.float32) for a in (project, expand, combine, short)]


def pack_kernel(owners, step_owners, slot_ref, map_ref, spec_ref, cw_ref, ker_ref, out_ref, rows, dest):
    step = pl.program_id(0)
    groups = map_ref.shape[0]
    count = groups * LANES
    width = spec_ref.shape[1]

    @pl.when(step == 0)
    def _():
        tile_map = map_ref[...]
        slot = jnp.zeros_like(tile_map)
        for t in range(owners * TILES):
            slot = jnp.where(tile_map == t, slot_ref[t], slot)
        owner = slot // TILES
        masks = jnp.concatenate(
            [(owner == o).astype(jnp.float32) for o in range(owners)], axis=0
        ).astype(jnp.bfloat16)
        size = owners * groups
        at0 = lax.broadcasted_iota(jnp.int32, (LANES, LANES), 0)
        at1 = lax.broadcasted_iota(jnp.int32, (LANES, LANES), 1)
        earlier = (at0 < at1).astype(jnp.float32).astype(jnp.bfloat16)
        ones = jnp.ones((LANES, LANES), jnp.bfloat16)
        r0 = lax.broadcasted_iota(jnp.int32, (size, size), 0)
        r1 = lax.broadcasted_iota(jnp.int32, (size, size), 1)
        above = jnp.logical_and(r0 // groups == r1 // groups, r1 < r0)
        above = above.astype(jnp.float32).astype(jnp.bfloat16)
        total = jnp.dot(masks, ones, preferred_element_type=jnp.float32).astype(jnp.bfloat16)
        rank = jnp.dot(masks, earlier, preferred_element_type=jnp.float32)
        rank = rank + jnp.dot(above, total, preferred_element_type=jnp.float32)
        place = jnp.zeros(owner.shape, jnp.float32)
        for o in range(owners):
            place = jnp.where(
                owner == o, rank[o * groups : (o + 1) * groups] + float(o * CAP), place
            )
        dest[...] = place.astype(jnp.int32)
        tile = (slot - owner * TILES + 1).astype(jnp.float32)
        turned = jnp.concatenate([tile] * (LANES // groups), axis=0).T
        for r in range(groups):
            column = jnp.broadcast_to(turned[:, r : r + 1], (LANES, LANES))
            rows[r * LANES : (r + 1) * LANES, 2 * width + LANES :] = column.astype(jnp.bfloat16)
        cw = cw_ref[...]
        weighted = cw.astype(jnp.float32) * spec_ref[...].astype(jnp.float32)
        rows[:, :width] = weighted.astype(jnp.bfloat16)
        rows[:, width : 2 * width] = cw
        rows[:, 2 * width : 2 * width + LANES] = ker_ref[...]

    amount = step_owners * CAP
    wanted = lax.broadcasted_iota(jnp.int32, (amount, LANES), 0) + step * amount
    chosen = jnp.concatenate(
        [
            (wanted == dest[r : r + 1, :]).astype(jnp.float32).astype(jnp.bfloat16)
            for r in range(groups)
        ],
        axis=1,
    )
    for half in range(2):
        got = jnp.dot(
            chosen, rows[:, half * width : (half + 1) * width], preferred_element_type=jnp.float32
        ).astype(jnp.bfloat16)
        for o in range(step_owners):
            for b in range(width // LANES):
                at = (half * (width // LANES) + b) * CAP
                out_ref[o, at : at + CAP, :] = got[
                    o * CAP : (o + 1) * CAP, b * LANES : (b + 1) * LANES
                ]
    got = jnp.dot(chosen, rows[:, 2 * width :], preferred_element_type=jnp.float32)
    at = 2 * width // LANES * CAP
    for o in range(step_owners):
        part = got[o * CAP : (o + 1) * CAP]
        out_ref[o, at : at + LANES, :] = part[:, :LANES].T.astype(jnp.bfloat16)
        out_ref[o, at + LANES : at + LANES + 16, :] = part[:, LANES:].T[:16].astype(jnp.bfloat16)


def grid_kernel(width, in_ref, project_ref, expand_ref, out_ref, total):
    step = pl.program_id(0)
    senders = in_ref.shape[0]
    blocks = 2 * width // LANES
    spectra = jnp.concatenate(
        [
            jnp.concatenate([in_ref[s, b * CAP : (b + 1) * CAP, :] for b in range(blocks)], axis=1)
            for s in range(senders)
        ],
        axis=0,
    )
    at = blocks * CAP
    columns = []
    for s in range(senders):
        kernel_cols = in_ref[s, at : at + LANES, :]
        tile = in_ref[s, at + LANES : at + LANES + 16, :].astype(jnp.float32)
        pieces = []
        for t in range(TILES):
            here = (tile == float(t + 1)).astype(jnp.float32).astype(jnp.bfloat16)
            pieces.append(kernel_cols * jnp.concatenate([here] * (LANES // 16), axis=0))
        columns.append(jnp.concatenate(pieces, axis=0))
    masked = jnp.concatenate(columns, axis=1)
    product = jnp.dot(masked, spectra, preferred_element_type=jnp.float32)

    @pl.when(step == 0)
    def _():
        total[...] = product

    @pl.when(step > 0)
    def _():
        total[...] += product

    @pl.when(step == pl.num_programs(0) - 1)
    def _():
        cube = total[:, :width] / (total[:, width:] + 1.0)
        coef = jnp.dot(cube, project_ref[...], precision=HIGHEST, preferred_element_type=jnp.float32)
        rest = cube - jnp.dot(
            coef, expand_ref[...], precision=HIGHEST, preferred_element_type=jnp.float32
        )
        rest = rest.astype(jnp.bfloat16)
        parts = out_ref.shape[0]
        mine = rest.shape[0] // parts
        turned = coef.T[:16]
        high = turned.astype(jnp.bfloat16).astype(jnp.float32)
        left = turned - high
        middle = left.astype(jnp.bfloat16).astype(jnp.float32)
        low = left - middle
        row = lax.broadcasted_iota(jnp.int32, turned.shape, 0)
        sent = jnp.where(row < BASIS, high, jnp.where(row < 2 * BASIS, middle, low))
        sent = jnp.where(row < 3 * BASIS, sent, 0.0)
        for c in range(parts):
            at = c * mine
            for b in range(width // LANES):
                out_ref[c, b * mine : (b + 1) * mine, :] = rest[
                    at : at + mine, b * LANES : (b + 1) * LANES
                ]
            group = sent[:, at // LANES * LANES : at // LANES * LANES + LANES]
            if at % LANES:
                group = pltpu.roll(group, LANES - at % LANES, axis=1)
            last = width // LANES * mine
            out_ref[c, last : last + 16, :] = group.astype(jnp.bfloat16)


def final_kernel(width, in_ref, combine_ref, short_ref, coef_ref, res_ref):
    parts = in_ref.shape[0]
    mine = res_ref.shape[0]
    last = width // LANES * mine
    sent = jnp.concatenate(
        [in_ref[c, last : last + 16, :].astype(jnp.float32) for c in range(parts)], axis=0
    )
    mixed = jnp.dot(combine_ref[...], sent, precision=HIGHEST, preferred_element_type=jnp.float32)
    coef_ref[...] = mixed[parts * 8 : parts * 8 + BASIS, :mine]
    turned = mixed[: parts * 8].T[:mine]
    for c in range(parts):
        rest = jnp.concatenate(
            [in_ref[c, b * mine : (b + 1) * mine, :] for b in range(width // LANES)], axis=1
        ).astype(jnp.float32)
        for k in range(BASIS):
            rest = rest + turned[:, c * 8 + k : c * 8 + k + 1] * short_ref[k : k + 1, :]
        res_ref[:, c * width : (c + 1) * width] = rest


def per_device(owners, parts, spectra, chan_weight, kernel, tile_map, tile_slot):
    count, width = spectra.shape
    pixels = TILES * LANES
    mine = pixels // parts
    project, expand, combine, short = (jnp.asarray(a) for a in tables(CHANNELS, parts))
    limit = pltpu.CompilerParams(vmem_limit_bytes=40 * 2**20)
    whole = lambda shape: pl.BlockSpec(shape, lambda i: (0,) * len(shape))

    long = 2 * width // LANES * CAP + LANES + 16
    at_once = 4
    packed = pl.pallas_call(
        functools.partial(pack_kernel, owners, at_once),
        grid=(owners // at_once,),
        out_shape=jax.ShapeDtypeStruct((owners, long, LANES), jnp.bfloat16),
        in_specs=[
            pl.BlockSpec(memory_space=pltpu.SMEM),
            whole((count // LANES, LANES)),
            whole((count, width)),
            whole((count, width)),
            whole((count, LANES)),
        ],
        out_specs=pl.BlockSpec((at_once, long, LANES), lambda i: (i, 0, 0)),
        scratch_shapes=[
            pltpu.VMEM((count, 2 * width + 2 * LANES), jnp.bfloat16),
            pltpu.VMEM((count // LANES, LANES), jnp.int32),
        ],
        compiler_params=limit,
    )(tile_slot, tile_map.reshape(count // LANES, LANES), spectra, chan_weight, kernel)

    routed = lax.all_to_all(packed, "scan", split_axis=0, concat_axis=0, tiled=True)

    tall = width // LANES * mine + 16
    gridded = pl.pallas_call(
        functools.partial(grid_kernel, width),
        grid=(owners // at_once,),
        out_shape=jax.ShapeDtypeStruct((parts, tall, LANES), jnp.bfloat16),
        in_specs=[
            pl.BlockSpec((at_once, long, LANES), lambda i: (i, 0, 0)),
            whole(project.shape),
            whole(expand.shape),
        ],
        out_specs=whole((parts, tall, LANES)),
        scratch_shapes=[pltpu.VMEM((pixels, 2 * width), jnp.float32)],
        compiler_params=limit,
    )(routed, project, expand)

    rows = lax.all_to_all(gridded, "chan", split_axis=0, concat_axis=0, tiled=True)

    return pl.pallas_call(
        functools.partial(final_kernel, width),
        out_shape=[
            jax.ShapeDtypeStruct((BASIS, mine), jnp.float32),
            jax.ShapeDtypeStruct((mine, CHANNELS), jnp.float32),
        ],
        compiler_params=limit,
    )(rows, combine, short)


def solution(mesh):
    placed = (P("scan", "chan"), P("scan", "chan"), P("scan", None), P("scan"), P())
    return jax.shard_map(
        functools.partial(per_device, mesh.shape["scan"], mesh.shape["chan"]),
        mesh=mesh,
        in_specs=placed,
        out_specs=(P(None, ("scan", "chan")), P(("scan", "chan"), None)),
        check_vma=False,
    )
```

time: 193 us -> 80.9 us (0.42)
  waiting for transfers between devices: 119 us -> 0 us
  blocking collectives: 0 us -> 64.5 us
  other arithmetic: 29.9 us -> 0 us
  between operations: 19.5 us -> 0.69 us
  matrix products: 14.4 us -> 0 us
  Pallas kernels: 0 us -> 11 us
  starting transfers between devices: 8.12 us -> 0 us
  local copies, waits for them, and re-layouts: 1.27 us -> 4.39 us
    reduce_scatter x1 -> x0, waiting for transfers between devices: 119 us -> none  [per_device(): lax.psum_scatter(grid_block(kernel_cols, stacked, slot_ids, tiles_owned *...]
    all_to_all x0 -> x2, blocking collectives: none -> 64.5 us  [the longest x1 41.3 us: per_device(): lax.all_to_all(packed, 'scan', split_axis=0, concat_axis=0, tiled=True)]
    reduce_sum x15 -> x0, other arithmetic: 21.8 us -> none  [the longest x10 12.1 us: basis_table(): column = column - jnp.sum(earlier * column) * earlier]
    dot_general x3 -> x0, matrix products: 14.4 us -> none  [the longest x1 12.4 us: grid_block(): product = jnp.dot(flattened, stacked, preferred_element_type=jnp.float32)]
    pallas_call x0 -> x3, Pallas kernels: none -> 11 us  [the longest x1 5.4 us: per_device(): pl.pallas_call(functools.partial(pack_kernel, owners, at_once), grid=(own...]
    all_to_all x1 -> x0, starting transfers between devices: 8.08 us -> none  [per_device(): lax.all_to_all(grid_cube, 'chan', split_axis=0, concat_axis=1, tiled=True)]
    div x3 -> x0, other arithmetic: 6.67 us -> none  [the longest x2 4.61 us: basis_table(): column = column / jnp.sqrt(jnp.sum(column * column))]
    unnamed x2 -> x18, local copies, waits for them, and re-layouts: 0.01 us -> 4.39 us
  transfers between devices with their start and end apart: 2 -> 0, of which waited for: 1 -> 0; matrix products, arithmetic and copies ran while one was open for 13% -> 0% of each run, Pallas kernels for 0% -> 0%
where the time goes in v1:
time: 80.9 us; the launch traced here: 80.6 us
  blocking collectives  64.5 us (80%)
  Pallas kernels  11 us (14%)
  local copies, waits for them, and re-layouts  4.39 us (5%)
    all_to_all x1, blocking collectives, per_device(): lax.all_to_all(packed, 'scan', split_axis=0, concat_axis=0, tiled=True)  41.3 us
    all_to_all x1, blocking collectives, per_device(): lax.all_to_all(gridded, 'chan', split_axis=0, concat_axis=0, tiled=True)  23.3 us
    pallas_call x1, Pallas kernels, per_device(): pl.pallas_call(functools.partial(pack_kernel, owners, at_once), grid=(own...  5.4 us
    unnamed x18, local copies, waits for them, and re-layouts  4.39 us
    pallas_call x1, Pallas kernels, per_device(): pl.pallas_call(functools.partial(grid_kernel, width), grid=(owners // at_...  3.91 us
    pallas_call x1, Pallas kernels, per_device(): pl.pallas_call(functools.partial(final_kernel, width), out_shape=[jax.Sha...  1.7 us

profile of v1, /device:TPU:1, one launch (start us, length us, event | category | flops | bytes accessed | tf_op | source)
XLA Modules:
  0.0 80.6 jit_solution(13638616530827515409)
XLA Ops:
  0.6 0.0 copy-start
  0.6 1.0 %copy-done = bf16[1024,256]{1,0:T(8,128)(2,1)S(1)} copy-done((bf16[1024,256]{1,0:T(8,128)(2,1)S(1)}, bf16[1024,256]{1,0:T(8,128)(2,1)}, u32[]{:S(2)}) %copy-start) | copy-done | bytes 524312
  1.7 0.0 copy-start.1
  1.7 1.0 %copy-done.1 = bf16[1024,256]{1,0:T(8,128)(2,1)S(1)} copy-done((bf16[1024,256]{1,0:T(8,128)(2,1)S(1)}, bf16[1024,256]{1,0:T(8,128)(2,1)}, u32[]{:S(2)}) %copy-start.1) | copy-done | bytes 524312
  2.7 0.0 copy-start.2
  2.7 0.9 %copy-done.2 = bf16[1024,128]{1,0:T(8,128)(2,1)S(1)} copy-done((bf16[1024,128]{1,0:T(8,128)(2,1)S(1)}, bf16[1024,128]{1,0:T(8,128)(2,1)}, u32[]{:S(2)}) %copy-start.2) | copy-done | bytes 262168
  3.7 0.0 copy-start.7
  3.7 0.7 copy-done.7
  4.4 0.0 copy-start.8
  4.4 0.7 copy-done.8
  5.0 5.4 %shard_map.104 = bf16[16,656,128]{2,1,0:T(8,128)(2,1)S(1)} custom-call(s32[64]{0:T(128)S(1)} %copy-done.8, s32[8,128]{1,0:T(8,128)S(1)} %bitcast.1, bf16[1024,256]{1,0:T(8,128)(2,1)S(1)} %copy-done, bf16[1024,256]{1,0:T(8,128)(2,1)S(1)} %copy-done.1, bf16[1024,128]{1,0:T(8,128)(2,1)S(1)} %copy-done.2), custom_call_target="tpu_custom_call" | custom-call | tf_op jit(solution)/shard_map/pallas_call | solution.py:216
  10.4 0.0 copy-start.4
  10.4 0.0 copy-start.5
  10.4 41.3 %all_to_all.10.in_ref = bf16[16,656,128]{2,1,0:T(8,128)(2,1)S(1)} all-to-all(bf16[16,656,128]{2,1,0:T(8,128)(2,1)S(1)} %shard_map.104), channel_id=1, replica_groups=mesh['scan'=16,'chan'=16] {'scan'}, dimensions={0} | all-to-all | bytes 5373952 | tf_op jit(solution)/shard_map/all_to_all | solution.py:235
  51.7 0.0 copy-done.4
  51.7 0.0 copy-done.5
  51.7 0.0 copy-start.3
  51.7 0.0 copy-start.6
  51.7 3.9 %shard_map.105 = bf16[16,80,128]{2,1,0:T(8,128)(2,1)S(1)} custom-call(bf16[16,656,128]{2,1,0:T(8,128)(2,1)S(1)} %all_to_all.10.in_ref, f32[256,128]{1,0:T(8,128)S(1)} %copy-done.5, f32[128,256]{1,0:T(8,128)S(1)} %copy-done.4), custom_call_target="tpu_custom_call" | custom-call | tf_op jit(solution)/shard_map/pallas_call | solution.py:238
  55.6 23.3 %all_to_all.11.in_ref = bf16[16,80,128]{2,1,0:T(8,128)(2,1)S(1)} all-to-all(bf16[16,80,128]{2,1,0:T(8,128)(2,1)S(1)} %shard_map.105), channel_id=1, replica_groups=mesh['scan'=16,'chan'=16] {'chan'}, dimensions={0} | all-to-all | bytes 655360 | tf_op jit(solution)/shard_map/all_to_all | solution.py:252
  78.9 0.0 copy-done.3
  78.9 0.0 copy-done.6
  78.9 1.7 %shard_map.106 = (f32[5,32]{1,0:T(8,128)}, f32[32,4096]{1,0:T(8,128)}) custom-call(bf16[16,80,128]{2,1,0:T(8,128)(2,1)S(1)} %all_to_all.11.in_ref, f32[136,256]{1,0:T(8,128)S(1)} %copy-done.3, f32[8,256]{1,0:T(8,128)S(1)} %copy-done.6), custom_call_target="tpu_custom_call" | custom-call | tf_op jit(solution)/shard_map/pallas_call | solution.py:254
Async XLA Ops:
  0.6 1.0 %copy-start = (bf16[1024,256]{1,0:T(8,128)(2,1)S(1)}, bf16[1024,256]{1,0:T(8,128)(2,1)}, u32[]{:S(2)}) copy-start(bf16[1024,256]{1,0:T(8,128)(2,1)} %spec_ref.1) | copy-start | bytes 1572868
  1.7 1.0 %copy-start.1 = (bf16[1024,256]{1,0:T(8,128)(2,1)S(1)}, bf16[1024,256]{1,0:T(8,128)(2,1)}, u32[]{:S(2)}) copy-start(bf16[1024,256]{1,0:T(8,128)(2,1)} %cw_ref.1) | copy-start | bytes 1572868
  2.7 0.9 %copy-start.2 = (bf16[1024,128]{1,0:T(8,128)(2,1)S(1)}, bf16[1024,128]{1,0:T(8,128)(2,1)}, u32[]{:S(2)}) copy-start(bf16[1024,128]{1,0:T(8,128)(2,1)} %ker_ref.1) | copy-start | bytes 786436
  3.7 0.7 copy-start.7
  4.4 0.7 copy-start.8
  10.4 41.3 %copy-start.4 = (f32[128,256]{1,0:T(8,128)S(1)}, f32[128,256]{1,0:T(8,128)}, u32[]{:S(2)}) copy-start(f32[128,256]{1,0:T(8,128)} %constant.9.clone.expand_ref) | copy-start | bytes 393220
  10.4 41.3 %copy-start.5 = (f32[256,128]{1,0:T(8,128)S(1)}, f32[256,128]{1,0:T(8,128)}, u32[]{:S(2)}) copy-start(f32[256,128]{1,0:T(8,128)} %constant.8.clone.project_ref) | copy-start | bytes 393220
  51.7 27.2 %copy-start.3 = (f32[136,256]{1,0:T(8,128)S(1)}, f32[136,256]{1,0:T(8,128)}, u32[]{:S(2)}) copy-start(f32[136,256]{1,0:T(8,128)} %constant.10.clone.combine_ref) | copy-start | bytes 417796
  51.7 27.2 %copy-start.6 = (f32[8,256]{1,0:T(8,128)S(1)}, f32[8,256]{1,0:T(8,128)}, u32[]{:S(2)}) copy-start(f32[8,256]{1,0:T(8,128)} %constant.11.clone.short_ref) | copy-start | bytes 24580

commit v2 on v0

v2 whole, which is shorter than its diff:
```python
import functools

import jax
import jax.numpy as jnp
import numpy as np
from jax import lax
from jax.experimental import pallas as pl
from jax.experimental.pallas import tpu as pltpu
from jax.sharding import PartitionSpec as P

CHANNELS = 4096
BASIS = 5
CAP = 128
TILES = 4
LANES = 128


def orthonormal(abscissa, terms):
    columns = []
    for degree in range(terms):
        column = abscissa**degree
        for earlier in columns:
            column = column - np.sum(earlier * column) * earlier
        columns.append(column / np.sqrt(np.sum(column * column)))
    return np.stack(columns, axis=1)


def split_terms(values, terms):
    left = np.asarray(values, np.float64)
    parts = []
    for _ in range(terms):
        part = left.astype(jnp.bfloat16)
        parts.append(part)
        left = left - part.astype(np.float64)
    return parts


LEFT = (0, 1, 2, 0, 0, 1)
RIGHT = (0, 0, 0, 1, 2, 1)


def tables(channels, parts):
    width = channels // parts
    basis = orthonormal((2.0 * np.arange(channels) + 1.0) / channels - 1.0, BASIS)
    local = orthonormal((2.0 * np.arange(width) + 1.0) / width - 1.0, BASIS)
    mix = np.stack([local.T @ basis[c * width : (c + 1) * width] for c in range(parts)])
    project = np.zeros((width, LANES))
    expand = np.zeros((LANES, width), jnp.bfloat16)
    terms = split_terms(local.T, 3)
    for group, term in enumerate(RIGHT):
        project[:, group * BASIS : (group + 1) * BASIS] = local
        expand[group * BASIS : (group + 1) * BASIS] = terms[term]
    project = np.concatenate(split_terms(project, 2), axis=1)
    combine = np.zeros((parts * 8 + 16, parts * 16))
    for c in range(parts):
        for copy in range(3):
            at = c * 16 + copy * BASIS
            combine[parts * 8 : parts * 8 + BASIS, at : at + BASIS] = mix[c].T
            combine[c * 8 : c * 8 + BASIS, at : at + BASIS] += np.eye(BASIS)
    for c in range(parts):
        combine[c * 8 : c * 8 + BASIS] -= mix[c] @ combine[parts * 8 : parts * 8 + BASIS]
    combine = np.concatenate(split_terms(combine, 3))
    short = np.zeros((parts, 8, width))
    short[:, :BASIS] = local.T
    short = split_terms(short.reshape(parts * 8, width), 2)
    short = np.concatenate([short[0], short[0], short[1]])
    return project, expand, combine, short


def dot(a, b):
    return jnp.dot(a, b, preferred_element_type=jnp.float32)


def one_hot(mask):
    return mask.astype(jnp.float32).astype(jnp.bfloat16)


def pack_kernel(
    owners, slot_hbm, map_hbm, spec_hbm, cw_hbm, ker_hbm, out_ref, slot_ref, map_ref, spec_ref, rows, sems
):
    groups = map_ref.shape[0]
    width = spec_ref.shape[1]
    copies = [
        pltpu.make_async_copy(slot_hbm, slot_ref, sems.at[0]),
        pltpu.make_async_copy(map_hbm, map_ref, sems.at[1]),
        pltpu.make_async_copy(spec_hbm, spec_ref, sems.at[2]),
        pltpu.make_async_copy(cw_hbm, rows.at[:, width : 2 * width], sems.at[3]),
        pltpu.make_async_copy(ker_hbm, rows.at[:, 2 * width : 2 * width + LANES], sems.at[4]),
    ]
    for copy in copies:
        copy.start()
    size = owners * groups
    at0 = lax.broadcasted_iota(jnp.int32, (LANES, LANES), 0)
    at1 = lax.broadcasted_iota(jnp.int32, (LANES, LANES), 1)
    earlier = one_hot(at0 < at1)
    ones = jnp.ones((LANES, LANES), jnp.bfloat16)
    r0 = lax.broadcasted_iota(jnp.int32, (size, size), 0)
    r1 = lax.broadcasted_iota(jnp.int32, (size, size), 1)
    above = one_hot(jnp.logical_and(r0 // groups == r1 // groups, r1 < r0))
    copies[0].wait()
    copies[1].wait()

    tile_map = map_ref[...]
    slot = jnp.zeros_like(tile_map)
    for t in range(owners * TILES):
        slot = jnp.where(tile_map == t, slot_ref[t], slot)
    owner = slot // TILES
    masks = jnp.concatenate(
        [(owner == o).astype(jnp.float32) for o in range(owners)], axis=0
    ).astype(jnp.bfloat16)
    total = dot(masks, ones).astype(jnp.bfloat16)
    rank = dot(masks, earlier) + dot(above, total)
    place = jnp.zeros(owner.shape, jnp.float32)
    for o in range(owners):
        place = jnp.where(owner == o, rank[o * groups : (o + 1) * groups] + float(o * CAP), place)
    place = place.astype(jnp.int32)
    tile = (slot - owner * TILES + 1).astype(jnp.float32)
    turned = jnp.concatenate([tile] * (LANES // groups), axis=0).T
    for r in range(groups):
        column = jnp.broadcast_to(turned[:, r : r + 1], (LANES, LANES))
        rows[r * LANES : (r + 1) * LANES, 2 * width + LANES :] = column.astype(jnp.bfloat16)

    at_once = 2
    amount = at_once * CAP
    at = 2 * width // LANES * CAP
    for step in range(owners // at_once):
        wanted = lax.broadcasted_iota(jnp.int32, (amount, LANES), 0) + step * amount
        chosen = jnp.concatenate(
            [one_hot(wanted == place[r : r + 1, :]) for r in range(groups)], axis=1
        )
        if step == 0:
            copies[2].wait()
            copies[3].wait()
            weighted = rows[:, width : 2 * width].astype(jnp.float32) * spec_ref[...].astype(jnp.float32)
            rows[:, :width] = weighted.astype(jnp.bfloat16)
            copies[4].wait()
        for half in range(2):
            got = dot(chosen, rows[:, half * width : (half + 1) * width]).astype(jnp.bfloat16)
            for o in range(at_once):
                for b in range(width // LANES):
                    to = (half * (width // LANES) + b) * CAP
                    out_ref[step * at_once + o, to : to + CAP, :] = got[
                        o * CAP : (o + 1) * CAP, b * LANES : (b + 1) * LANES
                    ]
        got = dot(chosen, rows[:, 2 * width :])
        for o in range(at_once):
            part = got[o * CAP : (o + 1) * CAP]
            to = step * at_once + o
            out_ref[to, at : at + LANES, :] = part[:, :LANES].T.astype(jnp.bfloat16)
            out_ref[to, at + LANES : at + LANES + 16, :] = part[:, LANES:].T[:16].astype(jnp.bfloat16)


def grid_kernel(width, in_ref, project_ref, expand_ref, out_ref):
    senders = in_ref.shape[0]
    blocks = 2 * width // LANES
    at_once = 4
    at = blocks * CAP
    parts = out_ref.shape[0]
    mine = TILES * LANES // parts
    last = width // LANES * mine
    total = None
    for first in range(0, senders, at_once):
        group = range(first, first + at_once)
        spectra = jnp.concatenate(
            [
                jnp.concatenate(
                    [in_ref[s, b * CAP : (b + 1) * CAP, :] for b in range(blocks)], axis=1
                )
                for s in group
            ],
            axis=0,
        )
        columns = []
        for s in group:
            kernel_cols = in_ref[s, at : at + LANES, :]
            tile = in_ref[s, at + LANES : at + LANES + 16, :].astype(jnp.float32)
            pieces = []
            for t in range(TILES):
                here = one_hot(tile == float(t + 1))
                pieces.append(kernel_cols * jnp.concatenate([here] * (LANES // 16), axis=0))
            columns.append(jnp.concatenate(pieces, axis=0))
        product = dot(jnp.concatenate(columns, axis=1), spectra)
        total = product if total is None else total + product

    cube = total[:, :width] / (total[:, width:] + 1.0)
    high = cube.astype(jnp.bfloat16)
    low = (cube - high.astype(jnp.float32)).astype(jnp.bfloat16)
    both = dot(high, project_ref[...])
    coef = both[:, :LANES] + (both[:, LANES:] + dot(low, project_ref[:, :LANES]))
    first = coef.astype(jnp.bfloat16).astype(jnp.float32)
    left = coef - first
    second = left.astype(jnp.bfloat16).astype(jnp.float32)
    third = left - second
    group = lax.broadcasted_iota(jnp.int32, coef.shape, 1) // BASIS
    terms = jnp.where(group == 2, third, first)
    terms = jnp.where(jnp.logical_or(group == 1, group == 5), second, terms)
    rest = (cube - dot(terms.astype(jnp.bfloat16), expand_ref[...])).astype(jnp.bfloat16)
    sent = terms.T[:16]
    pixels = TILES * LANES
    for at_pixel in range(0, pixels, mine):
        c = at_pixel // mine
        for b in range(width // LANES):
            out_ref[c, b * mine : (b + 1) * mine, :] = rest[
                at_pixel : at_pixel + mine, b * LANES : (b + 1) * LANES
            ]
        turned = sent[:, at_pixel // LANES * LANES : at_pixel // LANES * LANES + LANES]
        if at_pixel % LANES:
            turned = pltpu.roll(turned, LANES - at_pixel % LANES, axis=1)
        out_ref[c, last : last + 16, :] = turned.astype(jnp.bfloat16)


def final_kernel(width, in_ref, combine_ref, short_ref, coef_ref, res_ref):
    parts = in_ref.shape[0]
    mine = res_ref.shape[0]
    last = width // LANES * mine
    sent = jnp.concatenate([in_ref[c, last : last + 16, :] for c in range(parts)], axis=0)
    mixed = dot(combine_ref[...], sent)
    size = parts * 8 + 16
    mixed = mixed[:size] + (mixed[size : 2 * size] + mixed[2 * size :])
    coef_ref[...] = mixed[parts * 8 : parts * 8 + BASIS, :mine]
    turned = mixed[: parts * 8].T[:mine]
    high = turned.astype(jnp.bfloat16)
    low = (turned - high.astype(jnp.float32)).astype(jnp.bfloat16)
    both = jnp.concatenate([high, low, high], axis=1)
    owner = lax.broadcasted_iota(jnp.int32, both.shape, 1) % (parts * 8) // 8
    zero = jnp.zeros_like(both)
    spread = jnp.concatenate([jnp.where(owner == c, both, zero) for c in range(parts)], axis=0)
    added = dot(spread, short_ref[...])
    for c in range(parts):
        rest = jnp.concatenate(
            [in_ref[c, b * mine : (b + 1) * mine, :] for b in range(width // LANES)], axis=1
        ).astype(jnp.float32)
        res_ref[:, c * width : (c + 1) * width] = rest + added[c * mine : (c + 1) * mine]


def per_device(owners, parts, spectra, chan_weight, kernel, tile_map, tile_slot):
    count, width = spectra.shape
    mine = TILES * LANES // parts
    project, expand, combine, short = (jnp.asarray(a) for a in tables(CHANNELS, parts))
    limit = pltpu.CompilerParams(vmem_limit_bytes=40 * 2**20)
    hbm = pl.BlockSpec(memory_space=pltpu.HBM)

    long = 2 * width // LANES * CAP + LANES + 16
    packed = pl.pallas_call(
        functools.partial(pack_kernel, owners),
        out_shape=jax.ShapeDtypeStruct((owners, long, LANES), jnp.bfloat16),
        in_specs=[hbm] * 5,
        scratch_shapes=[
            pltpu.SMEM(tile_slot.shape, jnp.int32),
            pltpu.VMEM((count // LANES, LANES), jnp.int32),
            pltpu.VMEM((count, width), jnp.bfloat16),
            pltpu.VMEM((count, 2 * width + 2 * LANES), jnp.bfloat16),
            pltpu.SemaphoreType.DMA((5,)),
        ],
        compiler_params=limit,
    )(
        *[
            pltpu.with_memory_space_constraint(a, pltpu.HBM)
            for a in (
                tile_slot,
                tile_map.reshape(count // LANES, LANES),
                spectra,
                chan_weight,
                kernel,
            )
        ]
    )

    routed = lax.all_to_all(packed, "scan", split_axis=0, concat_axis=0, tiled=True)

    tall = width // LANES * mine + 16
    gridded = pl.pallas_call(
        functools.partial(grid_kernel, width),
        out_shape=jax.ShapeDtypeStruct((parts, tall, LANES), jnp.bfloat16),
        compiler_params=limit,
    )(routed, project, expand)

    rows = lax.all_to_all(gridded, "chan", split_axis=0, concat_axis=0, tiled=True)

    return pl.pallas_call(
        functools.partial(final_kernel, width),
        out_shape=[
            jax.ShapeDtypeStruct((BASIS, mine), jnp.float32),
            jax.ShapeDtypeStruct((mine, CHANNELS), jnp.float32),
        ],
        compiler_params=limit,
    )(rows, combine, short)


def solution(mesh):
    placed = (P("scan", "chan"), P("scan", "chan"), P("scan", None), P("scan"), P())
    return jax.shard_map(
        functools.partial(per_device, mesh.shape["scan"], mesh.shape["chan"]),
        mesh=mesh,
        in_specs=placed,
        out_specs=(P(None, ("scan", "chan")), P(("scan", "chan"), None)),
        check_vma=False,
    )
```

time: 193 us -> 73.4 us (0.38)
  waiting for transfers between devices: 119 us -> 0 us
  blocking collectives: 0 us -> 64.5 us
  other arithmetic: 29.9 us -> 0 us
  between operations: 19.5 us -> 0.67 us
  matrix products: 14.4 us -> 0 us
  starting transfers between devices: 8.12 us -> 0 us
  Pallas kernels: 0 us -> 7.95 us
    reduce_scatter x1 -> x0, waiting for transfers between devices: 119 us -> none  [per_device(): lax.psum_scatter(grid_block(kernel_cols, stacked, slot_ids, tiles_owned *...]
    all_to_all x0 -> x2, blocking collectives: none -> 64.5 us  [the longest x1 41.3 us: per_device(): lax.all_to_all(packed, 'scan', split_axis=0, concat_axis=0, tiled=True)]
    reduce_sum x15 -> x0, other arithmetic: 21.8 us -> none  [the longest x10 12.1 us: basis_table(): column = column - jnp.sum(earlier * column) * earlier]
    dot_general x3 -> x0, matrix products: 14.4 us -> none  [the longest x1 12.4 us: grid_block(): product = jnp.dot(flattened, stacked, preferred_element_type=jnp.float32)]
    all_to_all x1 -> x0, starting transfers between devices: 8.08 us -> none  [per_device(): lax.all_to_all(grid_cube, 'chan', split_axis=0, concat_axis=1, tiled=True)]
    pallas_call x0 -> x3, Pallas kernels: none -> 7.95 us  [the longest x1 4.91 us: per_device(): pl.pallas_call(functools.partial(pack_kernel, owners), out_shape=jax.Shap...]
    div x3 -> x0, other arithmetic: 6.67 us -> none  [the longest x2 4.61 us: basis_table(): column = column / jnp.sqrt(jnp.sum(column * column))]
  transfers between devices with their start and end apart: 2 -> 0, of which waited for: 1 -> 0; matrix products, arithmetic and copies ran while one was open for 13% -> 0% of each run, Pallas kernels for 0% -> 0%
where the time goes in v2:
time: 73.4 us; the launch traced here: 73.2 us
  blocking collectives  64.5 us (88%)
  Pallas kernels  7.95 us (11%)
    all_to_all x1, blocking collectives, per_device(): lax.all_to_all(packed, 'scan', split_axis=0, concat_axis=0, tiled=True)  41.3 us
    all_to_all x1, blocking collectives, per_device(): lax.all_to_all(gridded, 'chan', split_axis=0, concat_axis=0, tiled=True)  23.3 us
    pallas_call x1, Pallas kernels, per_device(): pl.pallas_call(functools.partial(pack_kernel, owners), out_shape=jax.Shap...  4.91 us
    pallas_call x1, Pallas kernels, per_device(): pl.pallas_call(functools.partial(grid_kernel, width), out_shape=jax.Shape...  1.61 us

profile of v2, /device:TPU:1, one launch (start us, length us, event | category | flops | bytes accessed | tf_op | source)
XLA Modules:
  0.0 73.2 jit_solution(11220886022477165409)
XLA Ops:
  0.6 4.9 %shard_map.104 = bf16[16,656,128]{2,1,0:T(8,128)(2,1)S(1)} custom-call(s32[64]{0:T(128)} %slot_hbm.1, s32[8,128]{1,0:T(8,128)} %bitcast.1, bf16[1024,256]{1,0:T(8,128)(2,1)} %spec_hbm.1, bf16[1024,256]{1,0:T(8,128)(2,1)} %cw_hbm.1, bf16[1024,128]{1,0:T(8,128)(2,1)} %ker_hbm.1), custom_call_target="tpu_custom_call" | custom-call | tf_op jit(solution)/shard_map/pallas_call | solution.py:244
  5.5 0.0 copy-start.2
  5.6 0.0 copy-start.3
  5.6 41.3 %all_to_all.10.in_ref = bf16[16,656,128]{2,1,0:T(8,128)(2,1)S(1)} all-to-all(bf16[16,656,128]{2,1,0:T(8,128)(2,1)S(1)} %shard_map.104), channel_id=1, replica_groups=mesh['scan'=16,'chan'=16] {'scan'}, dimensions={0} | all-to-all | bytes 5373952 | tf_op jit(solution)/shard_map/all_to_all | solution.py:269
  46.8 0.0 copy-done.2
  46.8 0.0 copy-done.3
  46.8 0.0 copy-start
  46.8 0.0 copy-start.1
  46.8 1.6 %shard_map.105 = bf16[16,80,128]{2,1,0:T(8,128)(2,1)S(1)} custom-call(bf16[16,656,128]{2,1,0:T(8,128)(2,1)S(1)} %all_to_all.10.in_ref, bf16[256,256]{1,0:T(8,128)(2,1)S(1)} %copy-done.2, bf16[128,256]{1,0:T(8,128)(2,1)S(1)} %copy-done.3), custom_call_target="tpu_custom_call" | custom-call | tf_op jit(solution)/shard_map/pallas_call | solution.py:272
  48.5 23.3 %all_to_all.11.in_ref = bf16[16,80,128]{2,1,0:T(8,128)(2,1)S(1)} all-to-all(bf16[16,80,128]{2,1,0:T(8,128)(2,1)S(1)} %shard_map.105), channel_id=1, replica_groups=mesh['scan'=16,'chan'=16] {'chan'}, dimensions={0} | all-to-all | bytes 655360 | tf_op jit(solution)/shard_map/all_to_all | solution.py:278
  71.7 0.0 copy-done
  71.7 0.0 copy-done.1
  71.7 1.4 %shard_map.106 = (f32[5,32]{1,0:T(8,128)}, f32[32,4096]{1,0:T(8,128)}) custom-call(bf16[16,80,128]{2,1,0:T(8,128)(2,1)S(1)} %all_to_all.11.in_ref, bf16[432,256]{1,0:T(8,128)(2,1)S(1)} %copy-done, bf16[384,256]{1,0:T(8,128)(2,1)S(1)} %copy-done.1), custom_call_target="tpu_custom_call" | custom-call | tf_op jit(solution)/shard_map/pallas_call | solution.py:280
Async XLA Ops:
  5.5 41.3 %copy-start.2 = (bf16[256,256]{1,0:T(8,128)(2,1)S(1)}, bf16[256,256]{1,0:T(8,128)(2,1)}, u32[]{:S(2)}) copy-start(bf16[256,256]{1,0:T(8,128)(2,1)} %constant.8.clone.project_ref) | copy-start | bytes 393220
  5.6 41.3 %copy-start.3 = (bf16[128,256]{1,0:T(8,128)(2,1)S(1)}, bf16[128,256]{1,0:T(8,128)(2,1)}, u32[]{:S(2)}) copy-start(bf16[128,256]{1,0:T(8,128)(2,1)} %constant.9.clone.expand_ref) | copy-start | bytes 196612
  46.8 24.9 %copy-start = (bf16[432,256]{1,0:T(8,128)(2,1)S(1)}, bf16[432,256]{1,0:T(8,128)(2,1)}, u32[]{:S(2)}) copy-start(bf16[432,256]{1,0:T(8,128)(2,1)} %constant.10.clone.combine_ref) | copy-start | bytes 663556
  46.8 24.9 %copy-start.1 = (bf16[384,256]{1,0:T(8,128)(2,1)S(1)}, bf16[384,256]{1,0:T(8,128)(2,1)}, u32[]{:S(2)}) copy-start(bf16[384,256]{1,0:T(8,128)(2,1)} %constant.11.clone.short_ref) | copy-start | bytes 589828

commit v3 on v2

--- a/solution.py
+++ b/solution.py
@@ -13,6 +13,8 @@
 CAP = 128
 TILES = 4
 LANES = 128
+ALIGN = 16
+HALF = LANES // 2
 
 
 def orthonormal(abscissa, terms):
@@ -76,16 +78,31 @@
 
 
 def pack_kernel(
-    owners, slot_hbm, map_hbm, spec_hbm, cw_hbm, ker_hbm, out_ref, slot_ref, map_ref, spec_ref, rows, sems
+    owners,
+    slot_hbm,
+    map_hbm,
+    spec_hbm,
+    cw_hbm,
+    ker_hbm,
+    out_ref,
+    slot_ref,
+    map_ref,
+    spec_ref,
+    rows,
+    ordered,
+    bounds,
+    limits,
+    sems,
 ):
+    core = lax.axis_index("chan") % 2
     groups = map_ref.shape[0]
     width = spec_ref.shape[1]
     copies = [
         pltpu.make_async_copy(slot_hbm, slot_ref, sems.at[0]),
         pltpu.make_async_copy(map_hbm, map_ref, sems.at[1]),
-        pltpu.make_async_copy(spec_hbm, spec_ref, sems.at[2]),
-        pltpu.make_async_copy(cw_hbm, rows.at[:, width : 2 * width], sems.at[3]),
-        pltpu.make_async_copy(ker_hbm, rows.at[:, 2 * width : 2 * width + LANES], sems.at[4]),
+        pltpu.make_async_copy(cw_hbm, rows.at[:, width : 2 * width], sems.at[2]),
+        pltpu.make_async_copy(ker_hbm, rows.at[:, 2 * width : 2 * width + LANES], sems.at[3]),
+        pltpu.make_async_copy(spec_hbm, spec_ref, sems.at[4]),
     ]
     for copy in copies:
         copy.start()
@@ -96,7 +113,9 @@
     ones = jnp.ones((LANES, LANES), jnp.bfloat16)
     r0 = lax.broadcasted_iota(jnp.int32, (size, size), 0)
     r1 = lax.broadcasted_iota(jnp.int32, (size, size), 1)
-    above = one_hot(jnp.logical_and(r0 // groups == r1 // groups, r1 < r0))
+    same = r0 // groups == r1 // groups
+    above = one_hot(jnp.logical_and(same, r1 < r0))
+    before = one_hot(r1 // groups < r0 // groups)
     copies[0].wait()
     copies[1].wait()
 
@@ -108,49 +127,64 @@
     masks = jnp.concatenate(
         [(owner == o).astype(jnp.float32) for o in range(owners)], axis=0
     ).astype(jnp.bfloat16)
-    total = dot(masks, ones).astype(jnp.bfloat16)
-    rank = dot(masks, earlier) + dot(above, total)
+    here = dot(masks, ones).astype(jnp.bfloat16)
+    rank = dot(masks, earlier) + dot(above, here)
+    count = dot(one_hot(same), here)
+    room = jnp.floor((count + (ALIGN - 1.0)) * (1.0 / ALIGN)) * (ALIGN / float(groups))
+    begin = dot(before, room.astype(jnp.bfloat16))
+    rank = rank + begin
     place = jnp.zeros(owner.shape, jnp.float32)
     for o in range(owners):
-        place = jnp.where(owner == o, rank[o * groups : (o + 1) * groups] + float(o * CAP), place)
+        place = jnp.where(owner == o, rank[o * groups : (o + 1) * groups], place)
     place = place.astype(jnp.int32)
+    table = jnp.where(at0 == at1 * groups, begin, 0.0)
+    table = table + jnp.where(at0 == (at1 - 64) * groups, count, 0.0)
+    bounds[...] = jnp.broadcast_to(
+        jnp.sum(table, axis=0, keepdims=True), bounds.shape
+    ).astype(jnp.int32)
+    fetch = pltpu.make_async_copy(bounds, limits, sems.at[5])
+    fetch.start()
     tile = (slot - owner * TILES + 1).astype(jnp.float32)
     turned = jnp.concatenate([tile] * (LANES // groups), axis=0).T
     for r in range(groups):
         column = jnp.broadcast_to(turned[:, r : r + 1], (LANES, LANES))
         rows[r * LANES : (r + 1) * LANES, 2 * width + LANES :] = column.astype(jnp.bfloat16)
 
-    at_once = 2
-    amount = at_once * CAP
-    at = 2 * width // LANES * CAP
-    for step in range(owners // at_once):
+    total = ordered.shape[0] - CAP
+    amount = 256
+    ordered[total:, :] = jnp.zeros((CAP, ordered.shape[1]), jnp.bfloat16)
+    for step in range(total // amount):
         wanted = lax.broadcasted_iota(jnp.int32, (amount, LANES), 0) + step * amount
         chosen = jnp.concatenate(
             [one_hot(wanted == place[r : r + 1, :]) for r in range(groups)], axis=1
         )
         if step == 0:
             copies[2].wait()
+            copies[4].wait()
+            weighted = rows[:, width : 2 * width].astype(jnp.float32)
+            weighted = weighted * spec_ref[...].astype(jnp.float32)
+            rows[:, :width] = weighted.astype(jnp.bfloat16)
             copies[3].wait()
-            weighted = rows[:, width : 2 * width].astype(jnp.float32) * spec_ref[...].astype(jnp.float32)
-            rows[:, :width] = weighted.astype(jnp.bfloat16)
-            copies[4].wait()
-        for half in range(2):
-            got = dot(chosen, rows[:, half * width : (half + 1) * width]).astype(jnp.bfloat16)
-            for o in range(at_once):
-                for b in range(width // LANES):
-                    to = (half * (width // LANES) + b) * CAP
-                    out_ref[step * at_once + o, to : to + CAP, :] = got[
-                        o * CAP : (o + 1) * CAP, b * LANES : (b + 1) * LANES
-                    ]
-        got = dot(chosen, rows[:, 2 * width :])
-        for o in range(at_once):
-            part = got[o * CAP : (o + 1) * CAP]
-            to = step * at_once + o
-            out_ref[to, at : at + LANES, :] = part[:, :LANES].T.astype(jnp.bfloat16)
-            out_ref[to, at + LANES : at + LANES + 16, :] = part[:, LANES:].T[:16].astype(jnp.bfloat16)
-
-
-def grid_kernel(width, in_ref, project_ref, expand_ref, out_ref):
+        ordered[step * amount : (step + 1) * amount, :] = dot(chosen, rows[...]).astype(jnp.bfloat16)
+    fetch.wait()
+    at = 2 * width // LANES * CAP
+    for o in range(owners):
+        window = pl.ds(pl.multiple_of(limits[0, o], ALIGN), CAP)
+        for b in range(2 * width // LANES):
+            out_ref[o, b * CAP : (b + 1) * CAP, :] = ordered[window, b * LANES : (b + 1) * LANES]
+        part = ordered[window, 2 * width :].astype(jnp.float32)
+        turned = part[:, :LANES].T
+        turned = jnp.where(core == 0, turned[:HALF], turned[HALF:])
+        out_ref[o, at : at + HALF, :] = turned.astype(jnp.bfloat16)
+        tiles = part[:, LANES:].T[:16]
+        slots = lax.broadcasted_iota(jnp.int32, tiles.shape, 1)
+        tiles = jnp.where(slots < limits[0, 64 + o], tiles, 0.0)
+        out_ref[o, at + HALF : at + HALF + 16, :] = tiles.astype(jnp.bfloat16)
+
+
+def grid_kernel(width, other, in_ref, cols_ref, project_ref, expand_ref, *refs):
+    out_ref = refs[-1]
+    half = (lax.axis_index("chan") + other) % 2
     senders = in_ref.shape[0]
     blocks = 2 * width // LANES
     at_once = 4
@@ -172,12 +206,12 @@
         )
         columns = []
         for s in group:
-            kernel_cols = in_ref[s, at : at + LANES, :]
-            tile = in_ref[s, at + LANES : at + LANES + 16, :].astype(jnp.float32)
+            kernel_cols = cols_ref[s]
+            tile = in_ref[s, at + HALF : at + HALF + 16, :].astype(jnp.float32)
             pieces = []
             for t in range(TILES):
                 here = one_hot(tile == float(t + 1))
-                pieces.append(kernel_cols * jnp.concatenate([here] * (LANES // 16), axis=0))
+                pieces.append(kernel_cols * jnp.concatenate([here] * (HALF // 16), axis=0))
             columns.append(jnp.concatenate(pieces, axis=0))
         product = dot(jnp.concatenate(columns, axis=1), spectra)
         total = product if total is None else total + product
@@ -196,9 +230,8 @@
     terms = jnp.where(jnp.logical_or(group == 1, group == 5), second, terms)
     rest = (cube - dot(terms.astype(jnp.bfloat16), expand_ref[...])).astype(jnp.bfloat16)
     sent = terms.T[:16]
-    pixels = TILES * LANES
-    for at_pixel in range(0, pixels, mine):
-        c = at_pixel // mine
+    for at_pixel in range(0, TILES * HALF, mine):
+        c = at_pixel // HALF * (LANES // mine) + half * (HALF // mine) + at_pixel % HALF // mine
         for b in range(width // LANES):
             out_ref[c, b * mine : (b + 1) * mine, :] = rest[
                 at_pixel : at_pixel + mine, b * LANES : (b + 1) * LANES
@@ -240,7 +273,8 @@
     limit = pltpu.CompilerParams(vmem_limit_bytes=40 * 2**20)
     hbm = pl.BlockSpec(memory_space=pltpu.HBM)
 
-    long = 2 * width // LANES * CAP + LANES + 16
+    long = 2 * width // LANES * CAP + HALF + 16
+    room = count + owners * ALIGN
     packed = pl.pallas_call(
         functools.partial(pack_kernel, owners),
         out_shape=jax.ShapeDtypeStruct((owners, long, LANES), jnp.bfloat16),
@@ -250,7 +284,10 @@
             pltpu.VMEM((count // LANES, LANES), jnp.int32),
             pltpu.VMEM((count, width), jnp.bfloat16),
             pltpu.VMEM((count, 2 * width + 2 * LANES), jnp.bfloat16),
-            pltpu.SemaphoreType.DMA((5,)),
+            pltpu.VMEM((room + CAP, 2 * width + 2 * LANES), jnp.bfloat16),
+            pltpu.VMEM((8, LANES), jnp.int32),
+            pltpu.SMEM((8, LANES), jnp.int32),
+            pltpu.SemaphoreType.DMA((6,)),
         ],
         compiler_params=limit,
     )(
@@ -269,11 +306,28 @@
     routed = lax.all_to_all(packed, "scan", split_axis=0, concat_axis=0, tiled=True)
 
     tall = width // LANES * mine + 16
+    at = 2 * width // LANES * CAP
+    mine_cols = routed[:, at : at + HALF, :]
+    other_cols = lax.ppermute(mine_cols, "chan", [(c, c ^ 1) for c in range(parts)])
+    whole = jax.ShapeDtypeStruct((parts, tall, LANES), jnp.bfloat16)
+    vmem = pl.BlockSpec(memory_space=pltpu.VMEM)
+    first = pl.pallas_call(
+        functools.partial(grid_kernel, width, 0),
+        out_shape=whole,
+        in_specs=[vmem] * 4,
+        out_specs=vmem,
+        compiler_params=limit,
+        cost_estimate=pl.CostEstimate(flops=10**9, bytes_accessed=3 * 10**6, transcendentals=0),
+    )(routed, mine_cols, project, expand)
     gridded = pl.pallas_call(
-        functools.partial(grid_kernel, width),
-        out_shape=jax.ShapeDtypeStruct((parts, tall, LANES), jnp.bfloat16),
+        functools.partial(grid_kernel, width, 1),
+        out_shape=whole,
+        in_specs=[vmem] * 5,
+        out_specs=vmem,
+        input_output_aliases={4: 0},
         compiler_params=limit,
-    )(routed, project, expand)
+        cost_estimate=pl.CostEstimate(flops=10**9, bytes_accessed=3 * 10**6, transcendentals=0),
+    )(routed, other_cols, project, expand, first)
 
     rows = lax.all_to_all(gridded, "chan", split_axis=0, concat_axis=0, tiled=True)
 

time: 73.4 us -> 71 us (0.967)
  blocking collectives: 64.5 us -> 60.3 us
  starting transfers between devices: 0 us -> 1.91 us
    all_to_all x1, blocking collectives: 41.3 us -> 38.5 us  [per_device(): lax.all_to_all(packed, 'scan', split_axis=0, concat_axis=0, tiled=True)]
    ppermute x0 -> x1, starting transfers between devices: none -> 1.91 us  [per_device(): lax.ppermute(mine_cols, 'chan', [(c, c ^ 1) for c in range(parts)])]
    all_to_all x1, blocking collectives: 23.3 us -> 21.7 us  [per_device(): lax.all_to_all(gridded, 'chan', split_axis=0, concat_axis=0, tiled=True)]
    pallas_call x1 -> x2, Pallas kernels: 1.61 us -> 2.07 us  [the longest x1 1.04 us: per_device(): pl.pallas_call(functools.partial(grid_kernel, width, 0), out_shape=whole,...]
  transfers between devices with their start and end apart: 0 -> 1, of which waited for: 0 -> 1; matrix products, arithmetic and copies ran while one was open for 0% -> 0% of each run, Pallas kernels for 0% -> 1%
where the time goes in v3:
time: 71 us; the launch traced here: 70.8 us
  blocking collectives  60.3 us (85%)
  Pallas kernels  7.77 us (11%)
  starting transfers between devices  1.91 us (3%)
    all_to_all x1, blocking collectives, per_device(): lax.all_to_all(packed, 'scan', split_axis=0, concat_axis=0, tiled=True)  38.5 us
    all_to_all x1, blocking collectives, per_device(): lax.all_to_all(gridded, 'chan', split_axis=0, concat_axis=0, tiled=True)  21.7 us
    pallas_call x1, Pallas kernels, per_device(): pl.pallas_call(functools.partial(pack_kernel, owners), out_shape=jax.Shap...  4.28 us
    ppermute x1, starting transfers between devices, per_device(): lax.ppermute(mine_cols, 'chan', [(c, c ^ 1) for c in range(parts)])  1.91 us
  transfers between devices with their start and end apart: 1, of which 1 were waited for; matrix products, arithmetic and copies ran while one was open for 0% of the time, Pallas kernels for 1%

profile of v3, /device:TPU:1, one launch (start us, length us, event | category | flops | bytes accessed | tf_op | source)
XLA Modules:
  0.0 70.8 jit_solution(8978020347973102250)
XLA Ops:
  0.6 4.3 %shard_map.104 = bf16[16,592,128]{2,1,0:T(8,128)(2,1)S(1)} custom-call(s32[64]{0:T(128)} %slot_hbm.1, s32[8,128]{1,0:T(8,128)} %bitcast.1, bf16[1024,256]{1,0:T(8,128)(2,1)} %spec_hbm.1, bf16[1024,256]{1,0:T(8,128)(2,1)} %cw_hbm.1, bf16[1024,128]{1,0:T(8,128)(2,1)} %ker_hbm.1), custom_call_target="tpu_custom_call" | custom-call | tf_op jit(solution)/shard_map/pallas_call | solution.py:278
  4.9 0.0 copy-start.2
  4.9 0.0 copy-start.3
  4.9 38.5 %all_to_all.10.in_ref = bf16[16,592,128]{2,1,0:T(8,128)(2,1)S(1)} all-to-all(bf16[16,592,128]{2,1,0:T(8,128)(2,1)S(1)} %shard_map.104), channel_id=1, replica_groups=mesh['scan'=16,'chan'=16] {'scan'}, dimensions={0} | all-to-all | bytes 4849664 | tf_op jit(solution)/shard_map/all_to_all | solution.py:306
  43.5 1.9 %collective-permute-start = (bf16[16,64,128]{2,1,0:T(8,128)(2,1)S(1)}, bf16[16,64,128]{2,1,0:T(8,128)(2,1)S(1)}, u32[]{:S(2)}, u32[]{:S(2)}) collective-permute-start(bf16[16,64,128]{2,1,0:T(8,128)(2,1)S(1)} %slice.4.cols_ref), channel_id=1, source_target_pairs={{0,1},{1,0},{2,3},{3,2},{4,5},{5,4},{6,7},{7,6},{8,9},{9,8},{10,11... | collective-permute-start | bytes 786440 | tf_op jit(solution)/shard_map/ppermute | solution.py:311
  45.4 0.0 copy-done.2
  45.4 0.0 copy-done.3
  45.4 1.0 %shard_map.105.refs_0_ = bf16[16,80,128]{2,1,0:T(8,128)(2,1)S(1)} custom-call(bf16[16,592,128]{2,1,0:T(8,128)(2,1)S(1)} %all_to_all.10.in_ref, bf16[16,64,128]{2,1,0:T(8,128)(2,1)S(1)} %slice.4.cols_ref, bf16[256,256]{1,0:T(8,128)(2,1)S(1)} %copy-done.2, bf16[128,256]{1,0:T(8,128)(2,1)S(1)} %copy-done.3), custom_call_target="tpu_custom_call" | custom-call | flops 1000000000 | bytes 3000000 | tf_op jit(solution)/shard_map/pallas_call | solution.py:314
  46.5 0.0 copy-start
  46.5 0.0 copy-start.1
  46.5 0.1 collective-permute-done.cols_ref
  46.6 1.0 %shard_map.106 = bf16[16,80,128]{2,1,0:T(8,128)(2,1)S(1)} custom-call(bf16[16,592,128]{2,1,0:T(8,128)(2,1)S(1)} %all_to_all.10.in_ref, bf16[16,64,128]{2,1,0:T(8,128)(2,1)S(1)} %collective-permute-done.cols_ref, bf16[256,256]{1,0:T(8,128)(2,1)S(1)} %copy-done.2, bf16[128,256]{1,0:T(8,128)(2,1)S(1)} %copy-done.3, ...), custom_call_target="tpu_custom_call", output_to_operand_aliasing={{}: (4, {})} | custom-call | flops 1000000000 | bytes 3000000 | tf_op jit(solution)/shard_map/pallas_call | solution.py:322
  47.6 21.7 %all_to_all.11.in_ref = bf16[16,80,128]{2,1,0:T(8,128)(2,1)S(1)} all-to-all(bf16[16,80,128]{2,1,0:T(8,128)(2,1)S(1)} %shard_map.106), channel_id=1, replica_groups=mesh['scan'=16,'chan'=16] {'chan'}, dimensions={0} | all-to-all | bytes 655360 | tf_op jit(solution)/shard_map/all_to_all | solution.py:332
  69.3 0.0 copy-done
  69.3 0.0 copy-done.1
  69.3 1.4 %shard_map.107 = (f32[5,32]{1,0:T(8,128)}, f32[32,4096]{1,0:T(8,128)}) custom-call(bf16[16,80,128]{2,1,0:T(8,128)(2,1)S(1)} %all_to_all.11.in_ref, bf16[432,256]{1,0:T(8,128)(2,1)S(1)} %copy-done, bf16[384,256]{1,0:T(8,128)(2,1)S(1)} %copy-done.1), custom_call_target="tpu_custom_call" | custom-call | tf_op jit(solution)/shard_map/pallas_call | solution.py:334
  (1 shorter events, 0.0 us)
Async XLA Ops:
  4.9 40.5 %copy-start.2 = (bf16[256,256]{1,0:T(8,128)(2,1)S(1)}, bf16[256,256]{1,0:T(8,128)(2,1)}, u32[]{:S(2)}) copy-start(bf16[256,256]{1,0:T(8,128)(2,1)} %constant.8.clone.project_ref) | copy-start | bytes 393220
  4.9 40.5 %copy-start.3 = (bf16[128,256]{1,0:T(8,128)(2,1)S(1)}, bf16[128,256]{1,0:T(8,128)(2,1)}, u32[]{:S(2)}) copy-start(bf16[128,256]{1,0:T(8,128)(2,1)} %constant.9.clone.expand_ref) | copy-start | bytes 196612
  43.5 3.1 %collective-permute-start = (bf16[16,64,128]{2,1,0:T(8,128)(2,1)S(1)}, bf16[16,64,128]{2,1,0:T(8,128)(2,1)S(1)}, u32[]{:S(2)}, u32[]{:S(2)}) collective-permute-start(bf16[16,64,128]{2,1,0:T(8,128)(2,1)S(1)} %slice.4.cols_ref), channel_id=1, source_target_pairs={{0,1},{1,0},{2,3},{3,2},{4,5},{5,4},{6,7},{7,6},{8,9},{9,8},{10,11... | collective-permute-start | bytes 786440 | tf_op jit(solution)/shard_map/ppermute | solution.py:311
  46.5 22.9 %copy-start = (bf16[432,256]{1,0:T(8,128)(2,1)S(1)}, bf16[432,256]{1,0:T(8,128)(2,1)}, u32[]{:S(2)}) copy-start(bf16[432,256]{1,0:T(8,128)(2,1)} %constant.10.clone.combine_ref) | copy-start | bytes 663556
  46.5 22.9 %copy-start.1 = (bf16[384,256]{1,0:T(8,128)(2,1)S(1)}, bf16[384,256]{1,0:T(8,128)(2,1)}, u32[]{:S(2)}) copy-start(bf16[384,256]{1,0:T(8,128)(2,1)} %constant.11.clone.short_ref) | copy-start | bytes 589828

commit v4 on v3

--- a/solution.py
+++ b/solution.py
@@ -61,6 +61,7 @@
             combine[c * 8 : c * 8 + BASIS, at : at + BASIS] += np.eye(BASIS)
     for c in range(parts):
         combine[c * 8 : c * 8 + BASIS] -= mix[c] @ combine[parts * 8 : parts * 8 + BASIS]
+    combine = combine.reshape(-1, parts, 2, 8).transpose(0, 2, 1, 3).reshape(-1, parts * 16)
     combine = np.concatenate(split_terms(combine, 3))
     short = np.zeros((parts, 8, width))
     short[:, :BASIS] = local.T
@@ -87,7 +88,6 @@
     out_ref,
     slot_ref,
     map_ref,
-    spec_ref,
     rows,
     ordered,
     bounds,
@@ -96,13 +96,13 @@
 ):
     core = lax.axis_index("chan") % 2
     groups = map_ref.shape[0]
-    width = spec_ref.shape[1]
+    width = spec_hbm.shape[1]
     copies = [
         pltpu.make_async_copy(slot_hbm, slot_ref, sems.at[0]),
         pltpu.make_async_copy(map_hbm, map_ref, sems.at[1]),
         pltpu.make_async_copy(cw_hbm, rows.at[:, width : 2 * width], sems.at[2]),
         pltpu.make_async_copy(ker_hbm, rows.at[:, 2 * width : 2 * width + LANES], sems.at[3]),
-        pltpu.make_async_copy(spec_hbm, spec_ref, sems.at[4]),
+        pltpu.make_async_copy(spec_hbm, rows.at[:, :width], sems.at[4]),
     ]
     for copy in copies:
         copy.start()
@@ -159,13 +159,12 @@
             [one_hot(wanted == place[r : r + 1, :]) for r in range(groups)], axis=1
         )
         if step == 0:
-            copies[2].wait()
-            copies[4].wait()
-            weighted = rows[:, width : 2 * width].astype(jnp.float32)
-            weighted = weighted * spec_ref[...].astype(jnp.float32)
-            rows[:, :width] = weighted.astype(jnp.bfloat16)
-            copies[3].wait()
-        ordered[step * amount : (step + 1) * amount, :] = dot(chosen, rows[...]).astype(jnp.bfloat16)
+            for copy in copies[2:]:
+                copy.wait()
+        got = dot(chosen, rows[...])
+        at = slice(step * amount, (step + 1) * amount)
+        ordered[at, :width] = (got[:, :width] * got[:, width : 2 * width]).astype(jnp.bfloat16)
+        ordered[at, width:] = got[:, width:].astype(jnp.bfloat16)
     fetch.wait()
     at = 2 * width // LANES * CAP
     for o in range(owners):
@@ -176,10 +175,10 @@
         turned = part[:, :LANES].T
         turned = jnp.where(core == 0, turned[:HALF], turned[HALF:])
         out_ref[o, at : at + HALF, :] = turned.astype(jnp.bfloat16)
-        tiles = part[:, LANES:].T[:16]
+        tiles = part[:, LANES:].T[:8]
         slots = lax.broadcasted_iota(jnp.int32, tiles.shape, 1)
         tiles = jnp.where(slots < limits[0, 64 + o], tiles, 0.0)
-        out_ref[o, at + HALF : at + HALF + 16, :] = tiles.astype(jnp.bfloat16)
+        out_ref[o, at + HALF : at + HALF + 8, :] = tiles.astype(jnp.bfloat16)
 
 
 def grid_kernel(width, other, in_ref, cols_ref, project_ref, expand_ref, *refs):
@@ -207,11 +206,12 @@
         columns = []
         for s in group:
             kernel_cols = cols_ref[s]
-            tile = in_ref[s, at + HALF : at + HALF + 16, :].astype(jnp.float32)
+            tile = in_ref[s, at + HALF : at + HALF + 8, :].astype(jnp.float32)
             pieces = []
             for t in range(TILES):
-                here = one_hot(tile == float(t + 1))
-                pieces.append(kernel_cols * jnp.concatenate([here] * (HALF // 16), axis=0))
+                here = (tile == float(t + 1)).astype(jnp.float32)
+                here = jnp.concatenate([here] * (HALF // 8), axis=0).astype(jnp.bfloat16)
+                pieces.append(kernel_cols * here)
             columns.append(jnp.concatenate(pieces, axis=0))
         product = dot(jnp.concatenate(columns, axis=1), spectra)
         total = product if total is None else total + product
@@ -230,23 +230,31 @@
     terms = jnp.where(jnp.logical_or(group == 1, group == 5), second, terms)
     rest = (cube - dot(terms.astype(jnp.bfloat16), expand_ref[...])).astype(jnp.bfloat16)
     sent = terms.T[:16]
+    lane = lax.broadcasted_iota(jnp.int32, (8, LANES), 1)
     for at_pixel in range(0, TILES * HALF, mine):
         c = at_pixel // HALF * (LANES // mine) + half * (HALF // mine) + at_pixel % HALF // mine
         for b in range(width // LANES):
             out_ref[c, b * mine : (b + 1) * mine, :] = rest[
                 at_pixel : at_pixel + mine, b * LANES : (b + 1) * LANES
             ]
-        turned = sent[:, at_pixel // LANES * LANES : at_pixel // LANES * LANES + LANES]
+        here = sent[:, at_pixel // LANES * LANES : at_pixel // LANES * LANES + LANES]
+        upper, lower = here[:8], here[8:]
         if at_pixel % LANES:
-            turned = pltpu.roll(turned, LANES - at_pixel % LANES, axis=1)
-        out_ref[c, last : last + 16, :] = turned.astype(jnp.bfloat16)
+            upper = pltpu.roll(upper, LANES - at_pixel % LANES, axis=1)
+        if at_pixel % LANES != mine:
+            lower = pltpu.roll(lower, (LANES + mine - at_pixel % LANES) % LANES, axis=1)
+        out_ref[c, last : last + 8, :] = jnp.where(lane < mine, upper, lower).astype(jnp.bfloat16)
 
 
 def final_kernel(width, in_ref, combine_ref, short_ref, coef_ref, res_ref):
     parts = in_ref.shape[0]
     mine = res_ref.shape[0]
     last = width // LANES * mine
-    sent = jnp.concatenate([in_ref[c, last : last + 16, :] for c in range(parts)], axis=0)
+    upper = jnp.concatenate(
+        [in_ref[c, last : last + 8, :].astype(jnp.float32) for c in range(parts)], axis=0
+    )
+    lower = pltpu.roll(upper, LANES - mine, axis=1)
+    sent = jnp.concatenate([upper, lower], axis=0).astype(jnp.bfloat16)
     mixed = dot(combine_ref[...], sent)
     size = parts * 8 + 16
     mixed = mixed[:size] + (mixed[size : 2 * size] + mixed[2 * size :])
@@ -273,7 +281,7 @@
     limit = pltpu.CompilerParams(vmem_limit_bytes=40 * 2**20)
     hbm = pl.BlockSpec(memory_space=pltpu.HBM)
 
-    long = 2 * width // LANES * CAP + HALF + 16
+    long = 2 * width // LANES * CAP + HALF + 8
     room = count + owners * ALIGN
     packed = pl.pallas_call(
         functools.partial(pack_kernel, owners),
@@ -282,7 +290,6 @@
         scratch_shapes=[
             pltpu.SMEM(tile_slot.shape, jnp.int32),
             pltpu.VMEM((count // LANES, LANES), jnp.int32),
-            pltpu.VMEM((count, width), jnp.bfloat16),
             pltpu.VMEM((count, 2 * width + 2 * LANES), jnp.bfloat16),
             pltpu.VMEM((room + CAP, 2 * width + 2 * LANES), jnp.bfloat16),
             pltpu.VMEM((8, LANES), jnp.int32),
@@ -305,7 +312,7 @@
 
     routed = lax.all_to_all(packed, "scan", split_axis=0, concat_axis=0, tiled=True)
 
-    tall = width // LANES * mine + 16
+    tall = width // LANES * mine + 8
     at = 2 * width // LANES * CAP
     mine_cols = routed[:, at : at + HALF, :]
     other_cols = lax.ppermute(mine_cols, "chan", [(c, c ^ 1) for c in range(parts)])

time: 71 us -> 69.8 us (0.983)
  blocking collectives: 60.3 us -> 59.2 us
where the time goes in v4:
time: 69.8 us; the launch traced here: 69.7 us
  blocking collectives  59.2 us (85%)
  Pallas kernels  7.73 us (11%)
  starting transfers between devices  1.91 us (3%)
  between operations  0.7 us (1%)
    all_to_all x1, blocking collectives, per_device(): lax.all_to_all(packed, 'scan', split_axis=0, concat_axis=0, tiled=True)  38.2 us
    all_to_all x1, blocking collectives, per_device(): lax.all_to_all(gridded, 'chan', split_axis=0, concat_axis=0, tiled=True)  21 us
    pallas_call x1, Pallas kernels, per_device(): pl.pallas_call(functools.partial(pack_kernel, owners), out_shape=jax.Shap...  4.16 us
    ppermute x1, starting transfers between devices, per_device(): lax.ppermute(mine_cols, 'chan', [(c, c ^ 1) for c in range(parts)])  1.91 us
    pallas_call x1, Pallas kernels, per_device(): pl.pallas_call(functools.partial(final_kernel, width), out_shape=[jax.Sha...  1.49 us
  transfers between devices with their start and end apart: 1, of which 1 were waited for; matrix products, arithmetic and copies ran while one was open for 0% of the time, Pallas kernels for 1%

profile of v4, /device:TPU:1, one launch (start us, length us, event | category | flops | bytes accessed | tf_op | source)
XLA Modules:
  0.0 69.7 jit_solution(16486530708710051095)
XLA Ops:
  0.6 4.2 %shard_map.104 = bf16[16,584,128]{2,1,0:T(8,128)(2,1)S(1)} custom-call(s32[64]{0:T(128)} %slot_hbm.1, s32[8,128]{1,0:T(8,128)} %bitcast.1, bf16[1024,256]{1,0:T(8,128)(2,1)} %spec_hbm.1, bf16[1024,256]{1,0:T(8,128)(2,1)} %cw_hbm.1, bf16[1024,128]{1,0:T(8,128)(2,1)} %ker_hbm.1), custom_call_target="tpu_custom_call" | custom-call | tf_op jit(solution)/shard_map/pallas_call | solution.py:286
  4.8 0.0 copy-start.2
  4.8 0.0 copy-start.3
  4.8 38.2 %all_to_all.10.in_ref = bf16[16,584,128]{2,1,0:T(8,128)(2,1)S(1)} all-to-all(bf16[16,584,128]{2,1,0:T(8,128)(2,1)S(1)} %shard_map.104), channel_id=1, replica_groups=mesh['scan'=16,'chan'=16] {'scan'}, dimensions={0} | all-to-all | bytes 4784128 | tf_op jit(solution)/shard_map/all_to_all | solution.py:313
  43.0 1.9 %collective-permute-start = (bf16[16,64,128]{2,1,0:T(8,128)(2,1)S(1)}, bf16[16,64,128]{2,1,0:T(8,128)(2,1)S(1)}, u32[]{:S(2)}, u32[]{:S(2)}) collective-permute-start(bf16[16,64,128]{2,1,0:T(8,128)(2,1)S(1)} %slice.4.cols_ref), channel_id=1, source_target_pairs={{0,1},{1,0},{2,3},{3,2},{4,5},{5,4},{6,7},{7,6},{8,9},{9,8},{10,11... | collective-permute-start | bytes 786440 | tf_op jit(solution)/shard_map/ppermute | solution.py:318
  45.0 0.0 copy-done.2
  45.0 0.0 copy-done.3
  45.0 1.0 %shard_map.105.refs_0_ = bf16[16,72,128]{2,1,0:T(8,128)(2,1)S(1)} custom-call(bf16[16,584,128]{2,1,0:T(8,128)(2,1)S(1)} %all_to_all.10.in_ref, bf16[16,64,128]{2,1,0:T(8,128)(2,1)S(1)} %slice.4.cols_ref, bf16[256,256]{1,0:T(8,128)(2,1)S(1)} %copy-done.2, bf16[128,256]{1,0:T(8,128)(2,1)S(1)} %copy-done.3), custom_call_target="tpu_custom_call" | custom-call | flops 1000000000 | bytes 3000000 | tf_op jit(solution)/shard_map/pallas_call | solution.py:321
  46.0 0.0 copy-start
  46.0 0.0 copy-start.1
  46.0 0.1 collective-permute-done.cols_ref
  46.1 1.0 %shard_map.106 = bf16[16,72,128]{2,1,0:T(8,128)(2,1)S(1)} custom-call(bf16[16,584,128]{2,1,0:T(8,128)(2,1)S(1)} %all_to_all.10.in_ref, bf16[16,64,128]{2,1,0:T(8,128)(2,1)S(1)} %collective-permute-done.cols_ref, bf16[256,256]{1,0:T(8,128)(2,1)S(1)} %copy-done.2, bf16[128,256]{1,0:T(8,128)(2,1)S(1)} %copy-done.3, ...), custom_call_target="tpu_custom_call", output_to_operand_aliasing={{}: (4, {})} | custom-call | flops 1000000000 | bytes 3000000 | tf_op jit(solution)/shard_map/pallas_call | solution.py:329
  47.2 21.0 %all_to_all.11.in_ref = bf16[16,72,128]{2,1,0:T(8,128)(2,1)S(1)} all-to-all(bf16[16,72,128]{2,1,0:T(8,128)(2,1)S(1)} %shard_map.106), channel_id=1, replica_groups=mesh['scan'=16,'chan'=16] {'chan'}, dimensions={0} | all-to-all | bytes 589824 | tf_op jit(solution)/shard_map/all_to_all | solution.py:339
  68.2 0.0 copy-done
  68.2 0.0 copy-done.1
  68.2 1.5 %shard_map.107 = (f32[5,32]{1,0:T(8,128)}, f32[32,4096]{1,0:T(8,128)}) custom-call(bf16[16,72,128]{2,1,0:T(8,128)(2,1)S(1)} %all_to_all.11.in_ref, bf16[432,256]{1,0:T(8,128)(2,1)S(1)} %copy-done, bf16[384,256]{1,0:T(8,128)(2,1)S(1)} %copy-done.1), custom_call_target="tpu_custom_call" | custom-call | tf_op jit(solution)/shard_map/pallas_call | solution.py:341
  (1 shorter events, 0.0 us)
Async XLA Ops:
  4.8 40.2 %copy-start.2 = (bf16[256,256]{1,0:T(8,128)(2,1)S(1)}, bf16[256,256]{1,0:T(8,128)(2,1)}, u32[]{:S(2)}) copy-start(bf16[256,256]{1,0:T(8,128)(2,1)} %constant.8.clone.project_ref) | copy-start | bytes 393220
  4.8 40.2 %copy-start.3 = (bf16[128,256]{1,0:T(8,128)(2,1)S(1)}, bf16[128,256]{1,0:T(8,128)(2,1)}, u32[]{:S(2)}) copy-start(bf16[128,256]{1,0:T(8,128)(2,1)} %constant.9.clone.expand_ref) | copy-start | bytes 196612
  43.0 3.1 %collective-permute-start = (bf16[16,64,128]{2,1,0:T(8,128)(2,1)S(1)}, bf16[16,64,128]{2,1,0:T(8,128)(2,1)S(1)}, u32[]{:S(2)}, u32[]{:S(2)}) collective-permute-start(bf16[16,64,128]{2,1,0:T(8,128)(2,1)S(1)} %slice.4.cols_ref), channel_id=1, source_target_pairs={{0,1},{1,0},{2,3},{3,2},{4,5},{5,4},{6,7},{7,6},{8,9},{9,8},{10,11... | collective-permute-start | bytes 786440 | tf_op jit(solution)/shard_map/ppermute | solution.py:318
  46.0 22.2 %copy-start = (bf16[432,256]{1,0:T(8,128)(2,1)S(1)}, bf16[432,256]{1,0:T(8,128)(2,1)}, u32[]{:S(2)}) copy-start(bf16[432,256]{1,0:T(8,128)(2,1)} %constant.10.clone.combine_ref) | copy-start | bytes 663556
  46.0 22.2 %copy-start.1 = (bf16[384,256]{1,0:T(8,128)(2,1)S(1)}, bf16[384,256]{1,0:T(8,128)(2,1)}, u32[]{:S(2)}) copy-start(bf16[384,256]{1,0:T(8,128)(2,1)} %constant.11.clone.short_ref) | copy-start | bytes 589828

commit v5 on v4

--- a/solution.py
+++ b/solution.py
@@ -89,6 +89,8 @@
     slot_ref,
     map_ref,
     rows,
+    chosen,
+    cols,
     ordered,
     bounds,
     limits,
@@ -100,8 +102,8 @@
     copies = [
         pltpu.make_async_copy(slot_hbm, slot_ref, sems.at[0]),
         pltpu.make_async_copy(map_hbm, map_ref, sems.at[1]),
-        pltpu.make_async_copy(cw_hbm, rows.at[:, width : 2 * width], sems.at[2]),
-        pltpu.make_async_copy(ker_hbm, rows.at[:, 2 * width : 2 * width + LANES], sems.at[3]),
+        pltpu.make_async_copy(ker_hbm, rows.at[:, 2 * width : 2 * width + LANES], sems.at[2]),
+        pltpu.make_async_copy(cw_hbm, rows.at[:, width : 2 * width], sems.at[3]),
         pltpu.make_async_copy(spec_hbm, rows.at[:, :width], sems.at[4]),
     ]
     for copy in copies:
@@ -150,28 +152,27 @@
         column = jnp.broadcast_to(turned[:, r : r + 1], (LANES, LANES))
         rows[r * LANES : (r + 1) * LANES, 2 * width + LANES :] = column.astype(jnp.bfloat16)
 
-    total = ordered.shape[0] - CAP
-    amount = 256
+    total = chosen.shape[0]
+    amount = 128
+    at = 2 * width // LANES * CAP
+    cols[total:, :] = jnp.zeros((CAP, cols.shape[1]), jnp.bfloat16)
     ordered[total:, :] = jnp.zeros((CAP, ordered.shape[1]), jnp.bfloat16)
+    copies[2].wait()
     for step in range(total // amount):
         wanted = lax.broadcasted_iota(jnp.int32, (amount, LANES), 0) + step * amount
-        chosen = jnp.concatenate(
+        picked = jnp.concatenate(
             [one_hot(wanted == place[r : r + 1, :]) for r in range(groups)], axis=1
         )
-        if step == 0:
-            for copy in copies[2:]:
-                copy.wait()
-        got = dot(chosen, rows[...])
-        at = slice(step * amount, (step + 1) * amount)
-        ordered[at, :width] = (got[:, :width] * got[:, width : 2 * width]).astype(jnp.bfloat16)
-        ordered[at, width:] = got[:, width:].astype(jnp.bfloat16)
+        here = slice(step * amount, (step + 1) * amount)
+        chosen[here, :] = picked
+        cols[here, :] = dot(picked, rows[:, 2 * width :]).astype(jnp.bfloat16)
     fetch.wait()
-    at = 2 * width // LANES * CAP
-    for o in range(owners):
+    copies[3].wait()
+    copies[4].wait()
+
+    def turn(o):
         window = pl.ds(pl.multiple_of(limits[0, o], ALIGN), CAP)
-        for b in range(2 * width // LANES):
-            out_ref[o, b * CAP : (b + 1) * CAP, :] = ordered[window, b * LANES : (b + 1) * LANES]
-        part = ordered[window, 2 * width :].astype(jnp.float32)
+        part = cols[window, :].astype(jnp.float32)
         turned = part[:, :LANES].T
         turned = jnp.where(core == 0, turned[:HALF], turned[HALF:])
         out_ref[o, at : at + HALF, :] = turned.astype(jnp.bfloat16)
@@ -179,6 +180,19 @@
         slots = lax.broadcasted_iota(jnp.int32, tiles.shape, 1)
         tiles = jnp.where(slots < limits[0, 64 + o], tiles, 0.0)
         out_ref[o, at + HALF : at + HALF + 8, :] = tiles.astype(jnp.bfloat16)
+
+    steps = total // amount
+    for step in range(steps):
+        here = slice(step * amount, (step + 1) * amount)
+        got = dot(chosen[here, :], rows[:, : 2 * width])
+        ordered[here, :width] = (got[:, :width] * got[:, width:]).astype(jnp.bfloat16)
+        ordered[here, width:] = got[:, width:].astype(jnp.bfloat16)
+        for o in range(step * owners // steps, (step + 1) * owners // steps):
+            turn(o)
+    for o in range(owners):
+        window = pl.ds(pl.multiple_of(limits[0, o], ALIGN), CAP)
+        for b in range(2 * width // LANES):
+            out_ref[o, b * CAP : (b + 1) * CAP, :] = ordered[window, b * LANES : (b + 1) * LANES]
 
 
 def grid_kernel(width, other, in_ref, cols_ref, project_ref, expand_ref, *refs):
@@ -246,7 +260,9 @@
         out_ref[c, last : last + 8, :] = jnp.where(lane < mine, upper, lower).astype(jnp.bfloat16)
 
 
-def final_kernel(width, in_ref, combine_ref, short_ref, coef_ref, res_ref):
+def final_kernel(
+    width, in_ref, combine_ref, short_ref, coef_hbm, res_hbm, coef_ref, res_ref, sems
+):
     parts = in_ref.shape[0]
     mine = res_ref.shape[0]
     last = width // LANES * mine
@@ -259,19 +275,33 @@
     size = parts * 8 + 16
     mixed = mixed[:size] + (mixed[size : 2 * size] + mixed[2 * size :])
     coef_ref[...] = mixed[parts * 8 : parts * 8 + BASIS, :mine]
+    copies = [pltpu.make_async_copy(coef_ref, coef_hbm, sems.at[0])]
+    copies[0].start()
     turned = mixed[: parts * 8].T[:mine]
     high = turned.astype(jnp.bfloat16)
     low = (turned - high.astype(jnp.float32)).astype(jnp.bfloat16)
     both = jnp.concatenate([high, low, high], axis=1)
     owner = lax.broadcasted_iota(jnp.int32, both.shape, 1) % (parts * 8) // 8
     zero = jnp.zeros_like(both)
-    spread = jnp.concatenate([jnp.where(owner == c, both, zero) for c in range(parts)], axis=0)
-    added = dot(spread, short_ref[...])
-    for c in range(parts):
-        rest = jnp.concatenate(
-            [in_ref[c, b * mine : (b + 1) * mine, :] for b in range(width // LANES)], axis=1
-        ).astype(jnp.float32)
-        res_ref[:, c * width : (c + 1) * width] = rest + added[c * mine : (c + 1) * mine]
+    pieces = sems.shape[0] - 1
+    for piece in range(pieces):
+        group = range(piece * parts // pieces, (piece + 1) * parts // pieces)
+        spread = jnp.concatenate([jnp.where(owner == c, both, zero) for c in group], axis=0)
+        added = dot(spread, short_ref[...])
+        for i, c in enumerate(group):
+            rest = jnp.concatenate(
+                [in_ref[c, b * mine : (b + 1) * mine, :] for b in range(width // LANES)], axis=1
+            ).astype(jnp.float32)
+            res_ref[:, c * width : (c + 1) * width] = rest + added[i * mine : (i + 1) * mine]
+        lanes = slice(group[0] * width, (group[-1] + 1) * width)
+        copies.append(
+            pltpu.make_async_copy(
+                res_ref.at[:, lanes], res_hbm.at[:, lanes], sems.at[piece + 1]
+            )
+        )
+        copies[-1].start()
+    for copy in copies:
+        copy.wait()
 
 
 def per_device(owners, parts, spectra, chan_weight, kernel, tile_map, tile_slot):
@@ -291,7 +321,9 @@
             pltpu.SMEM(tile_slot.shape, jnp.int32),
             pltpu.VMEM((count // LANES, LANES), jnp.int32),
             pltpu.VMEM((count, 2 * width + 2 * LANES), jnp.bfloat16),
-            pltpu.VMEM((room + CAP, 2 * width + 2 * LANES), jnp.bfloat16),
+            pltpu.VMEM((room, count), jnp.bfloat16),
+            pltpu.VMEM((room + CAP, 2 * LANES), jnp.bfloat16),
+            pltpu.VMEM((room + CAP, 2 * width), jnp.bfloat16),
             pltpu.VMEM((8, LANES), jnp.int32),
             pltpu.SMEM((8, LANES), jnp.int32),
             pltpu.SemaphoreType.DMA((6,)),
@@ -344,6 +376,12 @@
             jax.ShapeDtypeStruct((BASIS, mine), jnp.float32),
             jax.ShapeDtypeStruct((mine, CHANNELS), jnp.float32),
         ],
+        out_specs=[hbm, hbm],
+        scratch_shapes=[
+            pltpu.VMEM((BASIS, mine), jnp.float32),
+            pltpu.VMEM((mine, CHANNELS), jnp.float32),
+            pltpu.SemaphoreType.DMA((1 + 4,)),
+        ],
         compiler_params=limit,
     )(rows, combine, short)
 

time: 69.8 us -> 69.7 us (level)
  no operation moved by 1% of the time
where the time goes in v5:
time: 69.7 us; the launch traced here: 69.5 us
  blocking collectives  59.2 us (85%)
  Pallas kernels  7.58 us (11%)
  starting transfers between devices  1.91 us (3%)
  between operations  0.7 us (1%)
    all_to_all x1, blocking collectives, per_device(): lax.all_to_all(packed, 'scan', split_axis=0, concat_axis=0, tiled=True)  38.2 us
    all_to_all x1, blocking collectives, per_device(): lax.all_to_all(gridded, 'chan', split_axis=0, concat_axis=0, tiled=True)  21 us
    pallas_call x1, Pallas kernels, per_device(): pl.pallas_call(functools.partial(pack_kernel, owners), out_shape=jax.Shap...  4.08 us
    ppermute x1, starting transfers between devices, per_device(): lax.ppermute(mine_cols, 'chan', [(c, c ^ 1) for c in range(parts)])  1.91 us
    pallas_call x1, Pallas kernels, per_device(): pl.pallas_call(functools.partial(final_kernel, width), out_shape=[jax.Sha...  1.42 us
  transfers between devices with their start and end apart: 1, of which 1 were waited for; matrix products, arithmetic and copies ran while one was open for 0% of the time, Pallas kernels for 1%

profile of v5, /device:TPU:1, one launch (start us, length us, event | category | flops | bytes accessed | tf_op | source)
XLA Modules:
  0.0 69.5 jit_solution(67897862188969997)
XLA Ops:
  0.6 4.1 %shard_map.104 = bf16[16,584,128]{2,1,0:T(8,128)(2,1)S(1)} custom-call(s32[64]{0:T(128)} %slot_hbm.1, s32[8,128]{1,0:T(8,128)} %bitcast.1, bf16[1024,256]{1,0:T(8,128)(2,1)} %spec_hbm.1, bf16[1024,256]{1,0:T(8,128)(2,1)} %cw_hbm.1, bf16[1024,128]{1,0:T(8,128)(2,1)} %ker_hbm.1), custom_call_target="tpu_custom_call" | custom-call | tf_op jit(solution)/shard_map/pallas_call | solution.py:316
  4.7 0.0 copy-start.2
  4.7 0.0 copy-start.3
  4.7 38.2 %all_to_all.10.in_ref = bf16[16,584,128]{2,1,0:T(8,128)(2,1)S(1)} all-to-all(bf16[16,584,128]{2,1,0:T(8,128)(2,1)S(1)} %shard_map.104), channel_id=1, replica_groups=mesh['scan'=16,'chan'=16] {'scan'}, dimensions={0} | all-to-all | bytes 4784128 | tf_op jit(solution)/shard_map/all_to_all | solution.py:345
  43.0 1.9 %collective-permute-start = (bf16[16,64,128]{2,1,0:T(8,128)(2,1)S(1)}, bf16[16,64,128]{2,1,0:T(8,128)(2,1)S(1)}, u32[]{:S(2)}, u32[]{:S(2)}) collective-permute-start(bf16[16,64,128]{2,1,0:T(8,128)(2,1)S(1)} %slice.4.cols_ref), channel_id=1, source_target_pairs={{0,1},{1,0},{2,3},{3,2},{4,5},{5,4},{6,7},{7,6},{8,9},{9,8},{10,11... | collective-permute-start | bytes 786440 | tf_op jit(solution)/shard_map/ppermute | solution.py:350
  44.9 0.0 copy-done.2
  44.9 0.0 copy-done.3
  44.9 1.0 %shard_map.105.refs_0_ = bf16[16,72,128]{2,1,0:T(8,128)(2,1)S(1)} custom-call(bf16[16,584,128]{2,1,0:T(8,128)(2,1)S(1)} %all_to_all.10.in_ref, bf16[16,64,128]{2,1,0:T(8,128)(2,1)S(1)} %slice.4.cols_ref, bf16[256,256]{1,0:T(8,128)(2,1)S(1)} %copy-done.2, bf16[128,256]{1,0:T(8,128)(2,1)S(1)} %copy-done.3), custom_call_target="tpu_custom_call" | custom-call | flops 1000000000 | bytes 3000000 | tf_op jit(solution)/shard_map/pallas_call | solution.py:353
  45.9 0.0 copy-start
  45.9 0.0 copy-start.1
  45.9 0.1 collective-permute-done.cols_ref
  46.0 1.0 %shard_map.106 = bf16[16,72,128]{2,1,0:T(8,128)(2,1)S(1)} custom-call(bf16[16,584,128]{2,1,0:T(8,128)(2,1)S(1)} %all_to_all.10.in_ref, bf16[16,64,128]{2,1,0:T(8,128)(2,1)S(1)} %collective-permute-done.cols_ref, bf16[256,256]{1,0:T(8,128)(2,1)S(1)} %copy-done.2, bf16[128,256]{1,0:T(8,128)(2,1)S(1)} %copy-done.3, ...), custom_call_target="tpu_custom_call", output_to_operand_aliasing={{}: (4, {})} | custom-call | flops 1000000000 | bytes 3000000 | tf_op jit(solution)/shard_map/pallas_call | solution.py:361
  47.1 21.0 %all_to_all.11.in_ref = bf16[16,72,128]{2,1,0:T(8,128)(2,1)S(1)} all-to-all(bf16[16,72,128]{2,1,0:T(8,128)(2,1)S(1)} %shard_map.106), channel_id=1, replica_groups=mesh['scan'=16,'chan'=16] {'chan'}, dimensions={0} | all-to-all | bytes 589824 | tf_op jit(solution)/shard_map/all_to_all | solution.py:371
  68.1 0.0 copy-done
  68.1 0.0 copy-done.1
  68.1 1.4 %shard_map.107 = (f32[5,32]{1,0:T(8,128)}, f32[32,4096]{1,0:T(8,128)}) custom-call(bf16[16,72,128]{2,1,0:T(8,128)(2,1)S(1)} %all_to_all.11.in_ref, bf16[432,256]{1,0:T(8,128)(2,1)S(1)} %copy-done, bf16[384,256]{1,0:T(8,128)(2,1)S(1)} %copy-done.1), custom_call_target="tpu_custom_call" | custom-call | tf_op jit(solution)/shard_map/pallas_call | solution.py:373
  (1 shorter events, 0.0 us)
Async XLA Ops:
  4.7 40.2 %copy-start.2 = (bf16[256,256]{1,0:T(8,128)(2,1)S(1)}, bf16[256,256]{1,0:T(8,128)(2,1)}, u32[]{:S(2)}) copy-start(bf16[256,256]{1,0:T(8,128)(2,1)} %constant.8.clone.project_ref) | copy-start | bytes 393220
  4.7 40.1 %copy-start.3 = (bf16[128,256]{1,0:T(8,128)(2,1)S(1)}, bf16[128,256]{1,0:T(8,128)(2,1)}, u32[]{:S(2)}) copy-start(bf16[128,256]{1,0:T(8,128)(2,1)} %constant.9.clone.expand_ref) | copy-start | bytes 196612
  43.0 3.1 %collective-permute-start = (bf16[16,64,128]{2,1,0:T(8,128)(2,1)S(1)}, bf16[16,64,128]{2,1,0:T(8,128)(2,1)S(1)}, u32[]{:S(2)}, u32[]{:S(2)}) collective-permute-start(bf16[16,64,128]{2,1,0:T(8,128)(2,1)S(1)} %slice.4.cols_ref), channel_id=1, source_target_pairs={{0,1},{1,0},{2,3},{3,2},{4,5},{5,4},{6,7},{7,6},{8,9},{9,8},{10,11... | collective-permute-start | bytes 786440 | tf_op jit(solution)/shard_map/ppermute | solution.py:350
  45.9 22.2 %copy-start = (bf16[432,256]{1,0:T(8,128)(2,1)S(1)}, bf16[432,256]{1,0:T(8,128)(2,1)}, u32[]{:S(2)}) copy-start(bf16[432,256]{1,0:T(8,128)(2,1)} %constant.10.clone.combine_ref) | copy-start | bytes 663556
  45.9 22.2 %copy-start.1 = (bf16[384,256]{1,0:T(8,128)(2,1)S(1)}, bf16[384,256]{1,0:T(8,128)(2,1)}, u32[]{:S(2)}) copy-start(bf16[384,256]{1,0:T(8,128)(2,1)} %constant.11.clone.short_ref) | copy-start | bytes 589828

commit v6 on v5

--- a/solution.py
+++ b/solution.py
@@ -53,7 +53,7 @@
         project[:, group * BASIS : (group + 1) * BASIS] = local
         expand[group * BASIS : (group + 1) * BASIS] = terms[term]
     project = np.concatenate(split_terms(project, 2), axis=1)
-    combine = np.zeros((parts * 8 + 16, parts * 16))
+    combine = np.zeros((parts * 8 + LANES, parts * 16))
     for c in range(parts):
         for copy in range(3):
             at = c * 16 + copy * BASIS
@@ -62,7 +62,7 @@
     for c in range(parts):
         combine[c * 8 : c * 8 + BASIS] -= mix[c] @ combine[parts * 8 : parts * 8 + BASIS]
     combine = combine.reshape(-1, parts, 2, 8).transpose(0, 2, 1, 3).reshape(-1, parts * 16)
-    combine = np.concatenate(split_terms(combine, 3))
+    combine = np.concatenate(split_terms(combine.T, 3), axis=1)
     short = np.zeros((parts, 8, width))
     short[:, :BASIS] = local.T
     short = split_terms(short.reshape(parts * 8, width), 2)
@@ -269,15 +269,15 @@
     upper = jnp.concatenate(
         [in_ref[c, last : last + 8, :].astype(jnp.float32) for c in range(parts)], axis=0
     )
-    lower = pltpu.roll(upper, LANES - mine, axis=1)
-    sent = jnp.concatenate([upper, lower], axis=0).astype(jnp.bfloat16)
-    mixed = dot(combine_ref[...], sent)
-    size = parts * 8 + 16
-    mixed = mixed[:size] + (mixed[size : 2 * size] + mixed[2 * size :])
-    coef_ref[...] = mixed[parts * 8 : parts * 8 + BASIS, :mine]
+    turned = upper.T
+    sent = jnp.concatenate([turned[:mine], turned[mine : 2 * mine]], axis=1).astype(jnp.bfloat16)
+    mixed = dot(sent, combine_ref[...])
+    size = combine_ref.shape[1] // 3
+    mixed = mixed[:, :size] + (mixed[:, size : 2 * size] + mixed[:, 2 * size :])
+    coef_ref[...] = mixed[:, parts * 8 :].T[:BASIS]
     copies = [pltpu.make_async_copy(coef_ref, coef_hbm, sems.at[0])]
     copies[0].start()
-    turned = mixed[: parts * 8].T[:mine]
+    turned = mixed[:, : parts * 8]
     high = turned.astype(jnp.bfloat16)
     low = (turned - high.astype(jnp.float32)).astype(jnp.bfloat16)
     both = jnp.concatenate([high, low, high], axis=1)

time: 69.7 us -> 69.6 us (level)
  no operation moved by 1% of the time
where the time goes in v6:
time: 69.6 us; the launch traced here: 69.4 us
  blocking collectives  59.2 us (85%)
  Pallas kernels  7.45 us (11%)
  starting transfers between devices  1.91 us (3%)
  between operations  0.7 us (1%)
    all_to_all x1, blocking collectives, per_device(): lax.all_to_all(packed, 'scan', split_axis=0, concat_axis=0, tiled=True)  38.2 us
    all_to_all x1, blocking collectives, per_device(): lax.all_to_all(gridded, 'chan', split_axis=0, concat_axis=0, tiled=True)  21 us
    pallas_call x1, Pallas kernels, per_device(): pl.pallas_call(functools.partial(pack_kernel, owners), out_shape=jax.Shap...  4.08 us
    ppermute x1, starting transfers between devices, per_device(): lax.ppermute(mine_cols, 'chan', [(c, c ^ 1) for c in range(parts)])  1.91 us
  transfers between devices with their start and end apart: 1, of which 1 were waited for; matrix products, arithmetic and copies ran while one was open for 0% of the time, Pallas kernels for 1%

profile of v6, /device:TPU:1, one launch (start us, length us, event | category | flops | bytes accessed | tf_op | source)
XLA Modules:
  0.0 69.4 jit_solution(18413957709345605455)
XLA Ops:
  0.6 4.1 %shard_map.104 = bf16[16,584,128]{2,1,0:T(8,128)(2,1)S(1)} custom-call(s32[64]{0:T(128)} %slot_hbm.1, s32[8,128]{1,0:T(8,128)} %bitcast.1, bf16[1024,256]{1,0:T(8,128)(2,1)} %spec_hbm.1, bf16[1024,256]{1,0:T(8,128)(2,1)} %cw_hbm.1, bf16[1024,128]{1,0:T(8,128)(2,1)} %ker_hbm.1), custom_call_target="tpu_custom_call" | custom-call | tf_op jit(solution)/shard_map/pallas_call | solution.py:316
  4.7 0.0 copy-start.2
  4.7 0.0 copy-start.3
  4.7 38.2 %all_to_all.10.in_ref = bf16[16,584,128]{2,1,0:T(8,128)(2,1)S(1)} all-to-all(bf16[16,584,128]{2,1,0:T(8,128)(2,1)S(1)} %shard_map.104), channel_id=1, replica_groups=mesh['scan'=16,'chan'=16] {'scan'}, dimensions={0} | all-to-all | bytes 4784128 | tf_op jit(solution)/shard_map/all_to_all | solution.py:345
  43.0 1.9 %collective-permute-start = (bf16[16,64,128]{2,1,0:T(8,128)(2,1)S(1)}, bf16[16,64,128]{2,1,0:T(8,128)(2,1)S(1)}, u32[]{:S(2)}, u32[]{:S(2)}) collective-permute-start(bf16[16,64,128]{2,1,0:T(8,128)(2,1)S(1)} %slice.4.cols_ref), channel_id=1, source_target_pairs={{0,1},{1,0},{2,3},{3,2},{4,5},{5,4},{6,7},{7,6},{8,9},{9,8},{10,11... | collective-permute-start | bytes 786440 | tf_op jit(solution)/shard_map/ppermute | solution.py:350
  44.9 0.0 copy-done.2
  44.9 0.0 copy-done.3
  44.9 1.0 %shard_map.105.refs_0_ = bf16[16,72,128]{2,1,0:T(8,128)(2,1)S(1)} custom-call(bf16[16,584,128]{2,1,0:T(8,128)(2,1)S(1)} %all_to_all.10.in_ref, bf16[16,64,128]{2,1,0:T(8,128)(2,1)S(1)} %slice.4.cols_ref, bf16[256,256]{1,0:T(8,128)(2,1)S(1)} %copy-done.2, bf16[128,256]{1,0:T(8,128)(2,1)S(1)} %copy-done.3), custom_call_target="tpu_custom_call" | custom-call | flops 1000000000 | bytes 3000000 | tf_op jit(solution)/shard_map/pallas_call | solution.py:353
  45.9 0.0 copy-start
  45.9 0.0 copy-start.1
  46.0 0.1 collective-permute-done.cols_ref
  46.0 1.0 %shard_map.106 = bf16[16,72,128]{2,1,0:T(8,128)(2,1)S(1)} custom-call(bf16[16,584,128]{2,1,0:T(8,128)(2,1)S(1)} %all_to_all.10.in_ref, bf16[16,64,128]{2,1,0:T(8,128)(2,1)S(1)} %collective-permute-done.cols_ref, bf16[256,256]{1,0:T(8,128)(2,1)S(1)} %copy-done.2, bf16[128,256]{1,0:T(8,128)(2,1)S(1)} %copy-done.3, ...), custom_call_target="tpu_custom_call", output_to_operand_aliasing={{}: (4, {})} | custom-call | flops 1000000000 | bytes 3000000 | tf_op jit(solution)/shard_map/pallas_call | solution.py:361
  47.1 21.0 %all_to_all.11.in_ref = bf16[16,72,128]{2,1,0:T(8,128)(2,1)S(1)} all-to-all(bf16[16,72,128]{2,1,0:T(8,128)(2,1)S(1)} %shard_map.106), channel_id=1, replica_groups=mesh['scan'=16,'chan'=16] {'chan'}, dimensions={0} | all-to-all | bytes 589824 | tf_op jit(solution)/shard_map/all_to_all | solution.py:371
  68.1 0.0 copy-done
  68.1 0.0 copy-done.1
  68.1 1.3 %shard_map.107 = (f32[5,32]{1,0:T(8,128)}, f32[32,4096]{1,0:T(8,128)}) custom-call(bf16[16,72,128]{2,1,0:T(8,128)(2,1)S(1)} %all_to_all.11.in_ref, bf16[256,768]{1,0:T(8,128)(2,1)S(1)} %copy-done, bf16[384,256]{1,0:T(8,128)(2,1)S(1)} %copy-done.1), custom_call_target="tpu_custom_call" | custom-call | tf_op jit(solution)/shard_map/pallas_call | solution.py:373
  (1 shorter events, 0.0 us)
Async XLA Ops:
  4.7 40.2 %copy-start.2 = (bf16[256,256]{1,0:T(8,128)(2,1)S(1)}, bf16[256,256]{1,0:T(8,128)(2,1)}, u32[]{:S(2)}) copy-start(bf16[256,256]{1,0:T(8,128)(2,1)} %constant.8.clone.project_ref) | copy-start | bytes 393220
  4.7 40.2 %copy-start.3 = (bf16[128,256]{1,0:T(8,128)(2,1)S(1)}, bf16[128,256]{1,0:T(8,128)(2,1)}, u32[]{:S(2)}) copy-start(bf16[128,256]{1,0:T(8,128)(2,1)} %constant.9.clone.expand_ref) | copy-start | bytes 196612
  43.0 3.1 %collective-permute-start = (bf16[16,64,128]{2,1,0:T(8,128)(2,1)S(1)}, bf16[16,64,128]{2,1,0:T(8,128)(2,1)S(1)}, u32[]{:S(2)}, u32[]{:S(2)}) collective-permute-start(bf16[16,64,128]{2,1,0:T(8,128)(2,1)S(1)} %slice.4.cols_ref), channel_id=1, source_target_pairs={{0,1},{1,0},{2,3},{3,2},{4,5},{5,4},{6,7},{7,6},{8,9},{9,8},{10,11... | collective-permute-start | bytes 786440 | tf_op jit(solution)/shard_map/ppermute | solution.py:350
  45.9 22.2 %copy-start = (bf16[256,768]{1,0:T(8,128)(2,1)S(1)}, bf16[256,768]{1,0:T(8,128)(2,1)}, u32[]{:S(2)}) copy-start(bf16[256,768]{1,0:T(8,128)(2,1)} %constant.10.clone.combine_ref) | copy-start | bytes 1179652
  45.9 22.2 %copy-start.1 = (bf16[384,256]{1,0:T(8,128)(2,1)S(1)}, bf16[384,256]{1,0:T(8,128)(2,1)}, u32[]{:S(2)}) copy-start(bf16[384,256]{1,0:T(8,128)(2,1)} %constant.11.clone.short_ref) | copy-start | bytes 589828

commit v7 on v6

--- a/solution.py
+++ b/solution.py
@@ -122,9 +122,9 @@
     copies[1].wait()
 
     tile_map = map_ref[...]
-    slot = jnp.zeros_like(tile_map)
-    for t in range(owners * TILES):
-        slot = jnp.where(tile_map == t, slot_ref[t], slot)
+    table = jnp.concatenate([slot_ref[...], jnp.zeros_like(slot_ref[...])], axis=1)
+    table = jnp.broadcast_to(table, tile_map.shape)
+    slot = jnp.take_along_axis(table, tile_map, axis=1, mode="promise_in_bounds")
     owner = slot // TILES
     masks = jnp.concatenate(
         [(owner == o).astype(jnp.float32) for o in range(owners)], axis=0
@@ -280,14 +280,14 @@
     turned = mixed[:, : parts * 8]
     high = turned.astype(jnp.bfloat16)
     low = (turned - high.astype(jnp.float32)).astype(jnp.bfloat16)
-    both = jnp.concatenate([high, low, high], axis=1)
-    owner = lax.broadcasted_iota(jnp.int32, both.shape, 1) % (parts * 8) // 8
-    zero = jnp.zeros_like(both)
+    owner = lax.broadcasted_iota(jnp.int32, high.shape, 1) // 8
+    zero = jnp.zeros_like(high)
     pieces = sems.shape[0] - 1
     for piece in range(pieces):
         group = range(piece * parts // pieces, (piece + 1) * parts // pieces)
-        spread = jnp.concatenate([jnp.where(owner == c, both, zero) for c in group], axis=0)
-        added = dot(spread, short_ref[...])
+        highs = jnp.concatenate([jnp.where(owner == c, high, zero) for c in group], axis=0)
+        lows = jnp.concatenate([jnp.where(owner == c, low, zero) for c in group], axis=0)
+        added = dot(jnp.concatenate([highs, lows, highs], axis=1), short_ref[...])
         for i, c in enumerate(group):
             rest = jnp.concatenate(
                 [in_ref[c, b * mine : (b + 1) * mine, :] for b in range(width // LANES)], axis=1
@@ -318,7 +318,7 @@
         out_shape=jax.ShapeDtypeStruct((owners, long, LANES), jnp.bfloat16),
         in_specs=[hbm] * 5,
         scratch_shapes=[
-            pltpu.SMEM(tile_slot.shape, jnp.int32),
+            pltpu.VMEM((1, tile_slot.shape[0]), jnp.int32),
             pltpu.VMEM((count // LANES, LANES), jnp.int32),
             pltpu.VMEM((count, 2 * width + 2 * LANES), jnp.bfloat16),
             pltpu.VMEM((room, count), jnp.bfloat16),
@@ -333,7 +333,7 @@
         *[
             pltpu.with_memory_space_constraint(a, pltpu.HBM)
             for a in (
-                tile_slot,
+                tile_slot.reshape(1, -1),
                 tile_map.reshape(count // LANES, LANES),
                 spectra,
                 chan_weight,

time: 69.6 us -> 69.6 us (level)
  no operation moved by 1% of the time
where the time goes in v7:
time: 69.6 us; the launch traced here: 69.4 us
  blocking collectives  59.2 us (85%)
  Pallas kernels  7.47 us (11%)
  starting transfers between devices  1.91 us (3%)
  between operations  0.7 us (1%)
    all_to_all x1, blocking collectives, per_device(): lax.all_to_all(packed, 'scan', split_axis=0, concat_axis=0, tiled=True)  38.2 us
    all_to_all x1, blocking collectives, per_device(): lax.all_to_all(gridded, 'chan', split_axis=0, concat_axis=0, tiled=True)  21 us
    pallas_call x1, Pallas kernels, per_device(): pl.pallas_call(functools.partial(pack_kernel, owners), out_shape=jax.Shap...  4.1 us
    ppermute x1, starting transfers between devices, per_device(): lax.ppermute(mine_cols, 'chan', [(c, c ^ 1) for c in range(parts)])  1.91 us
  transfers between devices with their start and end apart: 1, of which 1 were waited for; matrix products, arithmetic and copies ran while one was open for 0% of the time, Pallas kernels for 1%

profile of v7, /device:TPU:1, one launch (start us, length us, event | category | flops | bytes accessed | tf_op | source)
XLA Modules:
  0.0 69.4 jit_solution(8342631121209229584)
XLA Ops:
  0.6 4.1 %shard_map.104 = bf16[16,584,128]{2,1,0:T(8,128)(2,1)S(1)} custom-call(s32[1,64]{1,0:T(1,128)} %bitcast.3, s32[8,128]{1,0:T(8,128)} %bitcast.2, bf16[1024,256]{1,0:T(8,128)(2,1)} %spec_hbm.1, bf16[1024,256]{1,0:T(8,128)(2,1)} %cw_hbm.1, bf16[1024,128]{1,0:T(8,128)(2,1)} %ker_hbm.1), custom_call_target="tpu_custom_call" | custom-call | tf_op jit(solution)/shard_map/pallas_call | solution.py:316
  4.7 0.0 copy-start.2
  4.8 0.0 copy-start.3
  4.8 38.2 %all_to_all.10.in_ref = bf16[16,584,128]{2,1,0:T(8,128)(2,1)S(1)} all-to-all(bf16[16,584,128]{2,1,0:T(8,128)(2,1)S(1)} %shard_map.104), channel_id=1, replica_groups=mesh['scan'=16,'chan'=16] {'scan'}, dimensions={0} | all-to-all | bytes 4784128 | tf_op jit(solution)/shard_map/all_to_all | solution.py:345
  43.0 1.9 %collective-permute-start = (bf16[16,64,128]{2,1,0:T(8,128)(2,1)S(1)}, bf16[16,64,128]{2,1,0:T(8,128)(2,1)S(1)}, u32[]{:S(2)}, u32[]{:S(2)}) collective-permute-start(bf16[16,64,128]{2,1,0:T(8,128)(2,1)S(1)} %slice.4.cols_ref), channel_id=1, source_target_pairs={{0,1},{1,0},{2,3},{3,2},{4,5},{5,4},{6,7},{7,6},{8,9},{9,8},{10,11... | collective-permute-start | bytes 786440 | tf_op jit(solution)/shard_map/ppermute | solution.py:350
  44.9 0.0 copy-done.2
  44.9 0.0 copy-done.3
  44.9 1.0 %shard_map.105.refs_0_ = bf16[16,72,128]{2,1,0:T(8,128)(2,1)S(1)} custom-call(bf16[16,584,128]{2,1,0:T(8,128)(2,1)S(1)} %all_to_all.10.in_ref, bf16[16,64,128]{2,1,0:T(8,128)(2,1)S(1)} %slice.4.cols_ref, bf16[256,256]{1,0:T(8,128)(2,1)S(1)} %copy-done.2, bf16[128,256]{1,0:T(8,128)(2,1)S(1)} %copy-done.3), custom_call_target="tpu_custom_call" | custom-call | flops 1000000000 | bytes 3000000 | tf_op jit(solution)/shard_map/pallas_call | solution.py:353
  46.0 0.0 copy-start
  46.0 0.0 copy-start.1
  46.0 0.1 collective-permute-done.cols_ref
  46.1 1.0 %shard_map.106 = bf16[16,72,128]{2,1,0:T(8,128)(2,1)S(1)} custom-call(bf16[16,584,128]{2,1,0:T(8,128)(2,1)S(1)} %all_to_all.10.in_ref, bf16[16,64,128]{2,1,0:T(8,128)(2,1)S(1)} %collective-permute-done.cols_ref, bf16[256,256]{1,0:T(8,128)(2,1)S(1)} %copy-done.2, bf16[128,256]{1,0:T(8,128)(2,1)S(1)} %copy-done.3, ...), custom_call_target="tpu_custom_call", output_to_operand_aliasing={{}: (4, {})} | custom-call | flops 1000000000 | bytes 3000000 | tf_op jit(solution)/shard_map/pallas_call | solution.py:361
  47.1 21.0 %all_to_all.11.in_ref = bf16[16,72,128]{2,1,0:T(8,128)(2,1)S(1)} all-to-all(bf16[16,72,128]{2,1,0:T(8,128)(2,1)S(1)} %shard_map.106), channel_id=1, replica_groups=mesh['scan'=16,'chan'=16] {'chan'}, dimensions={0} | all-to-all | bytes 589824 | tf_op jit(solution)/shard_map/all_to_all | solution.py:371
  68.1 0.0 copy-done
  68.1 0.0 copy-done.1
  68.1 1.3 %shard_map.107 = (f32[5,32]{1,0:T(8,128)}, f32[32,4096]{1,0:T(8,128)}) custom-call(bf16[16,72,128]{2,1,0:T(8,128)(2,1)S(1)} %all_to_all.11.in_ref, bf16[256,768]{1,0:T(8,128)(2,1)S(1)} %copy-done, bf16[384,256]{1,0:T(8,128)(2,1)S(1)} %copy-done.1), custom_call_target="tpu_custom_call" | custom-call | tf_op jit(solution)/shard_map/pallas_call | solution.py:373
  (1 shorter events, 0.0 us)
Async XLA Ops:
  4.7 40.2 %copy-start.2 = (bf16[256,256]{1,0:T(8,128)(2,1)S(1)}, bf16[256,256]{1,0:T(8,128)(2,1)}, u32[]{:S(2)}) copy-start(bf16[256,256]{1,0:T(8,128)(2,1)} %constant.8.clone.project_ref) | copy-start | bytes 393220
  4.8 40.2 %copy-start.3 = (bf16[128,256]{1,0:T(8,128)(2,1)S(1)}, bf16[128,256]{1,0:T(8,128)(2,1)}, u32[]{:S(2)}) copy-start(bf16[128,256]{1,0:T(8,128)(2,1)} %constant.9.clone.expand_ref) | copy-start | bytes 196612
  43.0 3.1 %collective-permute-start = (bf16[16,64,128]{2,1,0:T(8,128)(2,1)S(1)}, bf16[16,64,128]{2,1,0:T(8,128)(2,1)S(1)}, u32[]{:S(2)}, u32[]{:S(2)}) collective-permute-start(bf16[16,64,128]{2,1,0:T(8,128)(2,1)S(1)} %slice.4.cols_ref), channel_id=1, source_target_pairs={{0,1},{1,0},{2,3},{3,2},{4,5},{5,4},{6,7},{7,6},{8,9},{9,8},{10,11... | collective-permute-start | bytes 786440 | tf_op jit(solution)/shard_map/ppermute | solution.py:350
  46.0 22.2 %copy-start = (bf16[256,768]{1,0:T(8,128)(2,1)S(1)}, bf16[256,768]{1,0:T(8,128)(2,1)}, u32[]{:S(2)}) copy-start(bf16[256,768]{1,0:T(8,128)(2,1)} %constant.10.clone.combine_ref) | copy-start | bytes 1179652
  46.0 22.1 %copy-start.1 = (bf16[384,256]{1,0:T(8,128)(2,1)S(1)}, bf16[384,256]{1,0:T(8,128)(2,1)}, u32[]{:S(2)}) copy-start(bf16[384,256]{1,0:T(8,128)(2,1)} %constant.11.clone.short_ref) | copy-start | bytes 589828

commit v8 on v7

--- a/solution.py
+++ b/solution.py
@@ -181,6 +181,7 @@
         tiles = jnp.where(slots < limits[0, 64 + o], tiles, 0.0)
         out_ref[o, at + HALF : at + HALF + 8, :] = tiles.astype(jnp.bfloat16)
 
+    amount = 256
     steps = total // amount
     for step in range(steps):
         here = slice(step * amount, (step + 1) * amount)

time: 69.6 us -> 69.6 us (level)
  no operation moved by 1% of the time
where the time goes in v8:
time: 69.6 us; the launch traced here: 69.4 us
  blocking collectives  59.2 us (85%)
  Pallas kernels  7.44 us (11%)
  starting transfers between devices  1.91 us (3%)
  between operations  0.7 us (1%)
    all_to_all x1, blocking collectives, per_device(): lax.all_to_all(packed, 'scan', split_axis=0, concat_axis=0, tiled=True)  38.2 us
    all_to_all x1, blocking collectives, per_device(): lax.all_to_all(gridded, 'chan', split_axis=0, concat_axis=0, tiled=True)  21 us
    pallas_call x1, Pallas kernels, per_device(): pl.pallas_call(functools.partial(pack_kernel, owners), out_shape=jax.Shap...  4.07 us
    ppermute x1, starting transfers between devices, per_device(): lax.ppermute(mine_cols, 'chan', [(c, c ^ 1) for c in range(parts)])  1.91 us
  transfers between devices with their start and end apart: 1, of which 1 were waited for; matrix products, arithmetic and copies ran while one was open for 0% of the time, Pallas kernels for 1%

profile of v8, /device:TPU:1, one launch (start us, length us, event | category | flops | bytes accessed | tf_op | source)
XLA Modules:
  0.0 69.4 jit_solution(7737435488735640914)
XLA Ops:
  0.6 4.1 %shard_map.104 = bf16[16,584,128]{2,1,0:T(8,128)(2,1)S(1)} custom-call(s32[1,64]{1,0:T(1,128)} %bitcast.3, s32[8,128]{1,0:T(8,128)} %bitcast.2, bf16[1024,256]{1,0:T(8,128)(2,1)} %spec_hbm.1, bf16[1024,256]{1,0:T(8,128)(2,1)} %cw_hbm.1, bf16[1024,128]{1,0:T(8,128)(2,1)} %ker_hbm.1), custom_call_target="tpu_custom_call" | custom-call | tf_op jit(solution)/shard_map/pallas_call | solution.py:317
  4.7 0.0 copy-start.2
  4.7 0.0 copy-start.3
  4.7 38.2 %all_to_all.10.in_ref = bf16[16,584,128]{2,1,0:T(8,128)(2,1)S(1)} all-to-all(bf16[16,584,128]{2,1,0:T(8,128)(2,1)S(1)} %shard_map.104), channel_id=1, replica_groups=mesh['scan'=16,'chan'=16] {'scan'}, dimensions={0} | all-to-all | bytes 4784128 | tf_op jit(solution)/shard_map/all_to_all | solution.py:346
  43.0 1.9 %collective-permute-start = (bf16[16,64,128]{2,1,0:T(8,128)(2,1)S(1)}, bf16[16,64,128]{2,1,0:T(8,128)(2,1)S(1)}, u32[]{:S(2)}, u32[]{:S(2)}) collective-permute-start(bf16[16,64,128]{2,1,0:T(8,128)(2,1)S(1)} %slice.4.cols_ref), channel_id=1, source_target_pairs={{0,1},{1,0},{2,3},{3,2},{4,5},{5,4},{6,7},{7,6},{8,9},{9,8},{10,11... | collective-permute-start | bytes 786440 | tf_op jit(solution)/shard_map/ppermute | solution.py:351
  44.9 0.0 copy-done.2
  44.9 0.0 copy-done.3
  44.9 1.0 %shard_map.105.refs_0_ = bf16[16,72,128]{2,1,0:T(8,128)(2,1)S(1)} custom-call(bf16[16,584,128]{2,1,0:T(8,128)(2,1)S(1)} %all_to_all.10.in_ref, bf16[16,64,128]{2,1,0:T(8,128)(2,1)S(1)} %slice.4.cols_ref, bf16[256,256]{1,0:T(8,128)(2,1)S(1)} %copy-done.2, bf16[128,256]{1,0:T(8,128)(2,1)S(1)} %copy-done.3), custom_call_target="tpu_custom_call" | custom-call | flops 1000000000 | bytes 3000000 | tf_op jit(solution)/shard_map/pallas_call | solution.py:354
  45.9 0.0 copy-start
  45.9 0.0 copy-start.1
  45.9 0.1 collective-permute-done.cols_ref
  46.0 1.0 %shard_map.106 = bf16[16,72,128]{2,1,0:T(8,128)(2,1)S(1)} custom-call(bf16[16,584,128]{2,1,0:T(8,128)(2,1)S(1)} %all_to_all.10.in_ref, bf16[16,64,128]{2,1,0:T(8,128)(2,1)S(1)} %collective-permute-done.cols_ref, bf16[256,256]{1,0:T(8,128)(2,1)S(1)} %copy-done.2, bf16[128,256]{1,0:T(8,128)(2,1)S(1)} %copy-done.3, ...), custom_call_target="tpu_custom_call", output_to_operand_aliasing={{}: (4, {})} | custom-call | flops 1000000000 | bytes 3000000 | tf_op jit(solution)/shard_map/pallas_call | solution.py:362
  47.1 21.0 %all_to_all.11.in_ref = bf16[16,72,128]{2,1,0:T(8,128)(2,1)S(1)} all-to-all(bf16[16,72,128]{2,1,0:T(8,128)(2,1)S(1)} %shard_map.106), channel_id=1, replica_groups=mesh['scan'=16,'chan'=16] {'chan'}, dimensions={0} | all-to-all | bytes 589824 | tf_op jit(solution)/shard_map/all_to_all | solution.py:372
  68.1 0.0 copy-done
  68.1 0.0 copy-done.1
  68.1 1.3 %shard_map.107 = (f32[5,32]{1,0:T(8,128)}, f32[32,4096]{1,0:T(8,128)}) custom-call(bf16[16,72,128]{2,1,0:T(8,128)(2,1)S(1)} %all_to_all.11.in_ref, bf16[256,768]{1,0:T(8,128)(2,1)S(1)} %copy-done, bf16[384,256]{1,0:T(8,128)(2,1)S(1)} %copy-done.1), custom_call_target="tpu_custom_call" | custom-call | tf_op jit(solution)/shard_map/pallas_call | solution.py:374
  (1 shorter events, 0.0 us)
Async XLA Ops:
  4.7 40.2 %copy-start.2 = (bf16[256,256]{1,0:T(8,128)(2,1)S(1)}, bf16[256,256]{1,0:T(8,128)(2,1)}, u32[]{:S(2)}) copy-start(bf16[256,256]{1,0:T(8,128)(2,1)} %constant.8.clone.project_ref) | copy-start | bytes 393220
  4.7 40.2 %copy-start.3 = (bf16[128,256]{1,0:T(8,128)(2,1)S(1)}, bf16[128,256]{1,0:T(8,128)(2,1)}, u32[]{:S(2)}) copy-start(bf16[128,256]{1,0:T(8,128)(2,1)} %constant.9.clone.expand_ref) | copy-start | bytes 196612
  43.0 3.1 %collective-permute-start = (bf16[16,64,128]{2,1,0:T(8,128)(2,1)S(1)}, bf16[16,64,128]{2,1,0:T(8,128)(2,1)S(1)}, u32[]{:S(2)}, u32[]{:S(2)}) collective-permute-start(bf16[16,64,128]{2,1,0:T(8,128)(2,1)S(1)} %slice.4.cols_ref), channel_id=1, source_target_pairs={{0,1},{1,0},{2,3},{3,2},{4,5},{5,4},{6,7},{7,6},{8,9},{9,8},{10,11... | collective-permute-start | bytes 786440 | tf_op jit(solution)/shard_map/ppermute | solution.py:351
  45.9 22.2 %copy-start = (bf16[256,768]{1,0:T(8,128)(2,1)S(1)}, bf16[256,768]{1,0:T(8,128)(2,1)}, u32[]{:S(2)}) copy-start(bf16[256,768]{1,0:T(8,128)(2,1)} %constant.10.clone.combine_ref) | copy-start | bytes 1179652
  45.9 22.2 %copy-start.1 = (bf16[384,256]{1,0:T(8,128)(2,1)S(1)}, bf16[384,256]{1,0:T(8,128)(2,1)}, u32[]{:S(2)}) copy-start(bf16[384,256]{1,0:T(8,128)(2,1)} %constant.11.clone.short_ref) | copy-start | bytes 589828

commit v9 on v7

--- a/solution.py
+++ b/solution.py
@@ -62,7 +62,7 @@
     for c in range(parts):
         combine[c * 8 : c * 8 + BASIS] -= mix[c] @ combine[parts * 8 : parts * 8 + BASIS]
     combine = combine.reshape(-1, parts, 2, 8).transpose(0, 2, 1, 3).reshape(-1, parts * 16)
-    combine = np.concatenate(split_terms(combine.T, 3), axis=1)
+    combine = np.concatenate(split_terms(combine.T, 3), axis=0)
     short = np.zeros((parts, 8, width))
     short[:, :BASIS] = local.T
     short = split_terms(short.reshape(parts * 8, width), 2)
@@ -271,9 +271,7 @@
     )
     turned = upper.T
     sent = jnp.concatenate([turned[:mine], turned[mine : 2 * mine]], axis=1).astype(jnp.bfloat16)
-    mixed = dot(sent, combine_ref[...])
-    size = combine_ref.shape[1] // 3
-    mixed = mixed[:, :size] + (mixed[:, size : 2 * size] + mixed[:, 2 * size :])
+    mixed = dot(jnp.concatenate([sent] * 3, axis=1), combine_ref[...])
     coef_ref[...] = mixed[:, parts * 8 :].T[:BASIS]
     copies = [pltpu.make_async_copy(coef_ref, coef_hbm, sems.at[0])]
     copies[0].start()

time: 69.6 us -> 69.6 us (level)
  no operation moved by 1% of the time
where the time goes in v9:
time: 69.6 us; the launch traced here: 69.4 us
  blocking collectives  59.2 us (85%)
  Pallas kernels  7.49 us (11%)
  starting transfers between devices  1.91 us (3%)
  between operations  0.7 us (1%)
    all_to_all x1, blocking collectives, per_device(): lax.all_to_all(packed, 'scan', split_axis=0, concat_axis=0, tiled=True)  38.2 us
    all_to_all x1, blocking collectives, per_device(): lax.all_to_all(gridded, 'chan', split_axis=0, concat_axis=0, tiled=True)  21 us
    pallas_call x1, Pallas kernels, per_device(): pl.pallas_call(functools.partial(pack_kernel, owners), out_shape=jax.Shap...  4.12 us
    ppermute x1, starting transfers between devices, per_device(): lax.ppermute(mine_cols, 'chan', [(c, c ^ 1) for c in range(parts)])  1.91 us
  transfers between devices with their start and end apart: 1, of which 1 were waited for; matrix products, arithmetic and copies ran while one was open for 0% of the time, Pallas kernels for 1%

profile of v9, /device:TPU:1, one launch (start us, length us, event | category | flops | bytes accessed | tf_op | source)
XLA Modules:
  0.0 69.4 jit_solution(5710471329380968986)
XLA Ops:
  0.6 4.1 %shard_map.104 = bf16[16,584,128]{2,1,0:T(8,128)(2,1)S(1)} custom-call(s32[1,64]{1,0:T(1,128)} %bitcast.3, s32[8,128]{1,0:T(8,128)} %bitcast.2, bf16[1024,256]{1,0:T(8,128)(2,1)} %spec_hbm.1, bf16[1024,256]{1,0:T(8,128)(2,1)} %cw_hbm.1, bf16[1024,128]{1,0:T(8,128)(2,1)} %ker_hbm.1), custom_call_target="tpu_custom_call" | custom-call | tf_op jit(solution)/shard_map/pallas_call | solution.py:314
  4.8 0.0 copy-start.2
  4.8 0.0 copy-start.3
  4.8 38.2 %all_to_all.10.in_ref = bf16[16,584,128]{2,1,0:T(8,128)(2,1)S(1)} all-to-all(bf16[16,584,128]{2,1,0:T(8,128)(2,1)S(1)} %shard_map.104), channel_id=1, replica_groups=mesh['scan'=16,'chan'=16] {'scan'}, dimensions={0} | all-to-all | bytes 4784128 | tf_op jit(solution)/shard_map/all_to_all | solution.py:343
  43.0 1.9 %collective-permute-start = (bf16[16,64,128]{2,1,0:T(8,128)(2,1)S(1)}, bf16[16,64,128]{2,1,0:T(8,128)(2,1)S(1)}, u32[]{:S(2)}, u32[]{:S(2)}) collective-permute-start(bf16[16,64,128]{2,1,0:T(8,128)(2,1)S(1)} %slice.4.cols_ref), channel_id=1, source_target_pairs={{0,1},{1,0},{2,3},{3,2},{4,5},{5,4},{6,7},{7,6},{8,9},{9,8},{10,11... | collective-permute-start | bytes 786440 | tf_op jit(solution)/shard_map/ppermute | solution.py:348
  44.9 0.0 copy-done.2
  44.9 0.0 copy-done.3
  44.9 1.0 %shard_map.105.refs_0_ = bf16[16,72,128]{2,1,0:T(8,128)(2,1)S(1)} custom-call(bf16[16,584,128]{2,1,0:T(8,128)(2,1)S(1)} %all_to_all.10.in_ref, bf16[16,64,128]{2,1,0:T(8,128)(2,1)S(1)} %slice.4.cols_ref, bf16[256,256]{1,0:T(8,128)(2,1)S(1)} %copy-done.2, bf16[128,256]{1,0:T(8,128)(2,1)S(1)} %copy-done.3), custom_call_target="tpu_custom_call" | custom-call | flops 1000000000 | bytes 3000000 | tf_op jit(solution)/shard_map/pallas_call | solution.py:351
  46.0 0.0 copy-start
  46.0 0.0 copy-start.1
  46.0 0.1 collective-permute-done.cols_ref
  46.1 1.0 %shard_map.106 = bf16[16,72,128]{2,1,0:T(8,128)(2,1)S(1)} custom-call(bf16[16,584,128]{2,1,0:T(8,128)(2,1)S(1)} %all_to_all.10.in_ref, bf16[16,64,128]{2,1,0:T(8,128)(2,1)S(1)} %collective-permute-done.cols_ref, bf16[256,256]{1,0:T(8,128)(2,1)S(1)} %copy-done.2, bf16[128,256]{1,0:T(8,128)(2,1)S(1)} %copy-done.3, ...), custom_call_target="tpu_custom_call", output_to_operand_aliasing={{}: (4, {})} | custom-call | flops 1000000000 | bytes 3000000 | tf_op jit(solution)/shard_map/pallas_call | solution.py:359
  47.1 21.0 %all_to_all.11.in_ref = bf16[16,72,128]{2,1,0:T(8,128)(2,1)S(1)} all-to-all(bf16[16,72,128]{2,1,0:T(8,128)(2,1)S(1)} %shard_map.106), channel_id=1, replica_groups=mesh['scan'=16,'chan'=16] {'chan'}, dimensions={0} | all-to-all | bytes 589824 | tf_op jit(solution)/shard_map/all_to_all | solution.py:369
  68.1 0.0 copy-done
  68.1 0.0 copy-done.1
  68.1 1.3 %shard_map.107 = (f32[5,32]{1,0:T(8,128)}, f32[32,4096]{1,0:T(8,128)}) custom-call(bf16[16,72,128]{2,1,0:T(8,128)(2,1)S(1)} %all_to_all.11.in_ref, bf16[768,256]{1,0:T(8,128)(2,1)S(1)} %copy-done, bf16[384,256]{1,0:T(8,128)(2,1)S(1)} %copy-done.1), custom_call_target="tpu_custom_call" | custom-call | tf_op jit(solution)/shard_map/pallas_call | solution.py:371
  (1 shorter events, 0.0 us)
Async XLA Ops:
  4.8 40.1 %copy-start.2 = (bf16[256,256]{1,0:T(8,128)(2,1)S(1)}, bf16[256,256]{1,0:T(8,128)(2,1)}, u32[]{:S(2)}) copy-start(bf16[256,256]{1,0:T(8,128)(2,1)} %constant.8.clone.project_ref) | copy-start | bytes 393220
  4.8 40.1 %copy-start.3 = (bf16[128,256]{1,0:T(8,128)(2,1)S(1)}, bf16[128,256]{1,0:T(8,128)(2,1)}, u32[]{:S(2)}) copy-start(bf16[128,256]{1,0:T(8,128)(2,1)} %constant.9.clone.expand_ref) | copy-start | bytes 196612
  43.0 3.1 %collective-permute-start = (bf16[16,64,128]{2,1,0:T(8,128)(2,1)S(1)}, bf16[16,64,128]{2,1,0:T(8,128)(2,1)S(1)}, u32[]{:S(2)}, u32[]{:S(2)}) collective-permute-start(bf16[16,64,128]{2,1,0:T(8,128)(2,1)S(1)} %slice.4.cols_ref), channel_id=1, source_target_pairs={{0,1},{1,0},{2,3},{3,2},{4,5},{5,4},{6,7},{7,6},{8,9},{9,8},{10,11... | collective-permute-start | bytes 786440 | tf_op jit(solution)/shard_map/ppermute | solution.py:348
  46.0 22.2 %copy-start = (bf16[768,256]{1,0:T(8,128)(2,1)S(1)}, bf16[768,256]{1,0:T(8,128)(2,1)}, u32[]{:S(2)}) copy-start(bf16[768,256]{1,0:T(8,128)(2,1)} %constant.10.clone.combine_ref) | copy-start | bytes 1179652
  46.0 22.2 %copy-start.1 = (bf16[384,256]{1,0:T(8,128)(2,1)S(1)}, bf16[384,256]{1,0:T(8,128)(2,1)}, u32[]{:S(2)}) copy-start(bf16[384,256]{1,0:T(8,128)(2,1)} %constant.11.clone.short_ref) | copy-start | bytes 589828
